TPU v7x, 32 devices: a whole 2x2x4 slice. The times are simulated.
32 devices in a mesh: dp: 4 (over y, x), fsdp: 8 (over z, core).
Axes of the slice: x: 2, y: 2, z: 4, core: 2. Of those that a mesh axis runs over, the one named last changes fastest.
Arguments:
- x_short: bfloat16 [256, 128, 768], P(('dp', 'fsdp')), may hold values from -6 to 6
- x_long: bfloat16 [64, 512, 768], P(('dp', 'fsdp')), may hold values from -6 to 6
- cot_short: bfloat16 [256, 128, 768], P(('dp', 'fsdp')), may hold values from -6 to 6
- cot_long: bfloat16 [64, 512, 768], P(('dp', 'fsdp')), may hold values from -6 to 6
- logit_cot_short: float32 [256, 14], P(('dp', 'fsdp'))
- logit_cot_long: float32 [64, 14], P(('dp', 'fsdp'))
- len_short: int32 [256], P(('dp', 'fsdp')), may hold values from 64 to 128, as said below
- len_long: int32 [64], P(('dp', 'fsdp')), may hold values from 256 to 512, as said below
- block_slot: int32 [439], replicated, may hold values from 0 to 439, as said below
- master: float32 [440, 128, 128], P('fsdp')
- left_stat: float32 [440, 128, 128], P('fsdp'), as said below
- right_stat: float32 [440, 128, 128], P('fsdp'), as said below
- left_root: float32 [440, 128, 128], P('fsdp'), as said below
- right_root: float32 [440, 128, 128], P('fsdp'), as said below
- small_params: float32 [11406], replicated
- small_first: float32 [11406], replicated
- small_second: float32 [11406], replicated, as said below
Outputs:
- encoded_short: bfloat16 [256, 128, 768], P(('dp', 'fsdp'))
- logits_short: float32 [256, 14], P(('dp', 'fsdp'))
- encoded_long: bfloat16 [64, 512, 768], P(('dp', 'fsdp'))
- logits_long: float32 [64, 14], P(('dp', 'fsdp'))
- input_grad_short: float32 [256, 128, 768], P(('dp', 'fsdp'))
- input_grad_long: float32 [64, 512, 768], P(('dp', 'fsdp'))
- slot_grad: float32 [440, 128, 128], P('fsdp')
- new_left: float32 [440, 128, 128], P('fsdp')
- new_right: float32 [440, 128, 128], P('fsdp')
- new_master: float32 [440, 128, 128], P('fsdp')
- new_first: float32 [11406], replicated
- new_second: float32 [11406], replicated
- new_small: float32 [11406], replicated
Inputs may be any that keep to these rules, and one draw needn't show every extreme that they name: `len_short`: each sequence's tokens fill its first positions; some sequence of every draw fills all 128. `len_long`: each sequence's tokens fill its first positions; some sequence of every draw fills all 512. `block_slot`: all different; slot s lies on index s // 55 of fsdp; the slots that no block names hold no block. `left_stat`: symmetric in every slot. `right_stat`: symmetric in every slot. `left_root`: symmetric in every slot. `right_root`: symmetric in every slot. `small_second`: positive.
All inputs are finite; a program needn't handle non-finite values.
Results may differ from a plain program's by a relative error of at most 0.014.
The roundings to bfloat16 on the way count: a program that leaves them out, or rounds other values in their place, can miss the bound.
Values may be sent and summed in bfloat16 or wider, within the bound.
A program may use at most 320 MiB of HBM per device.

v0:
```python
from functools import partial

import jax
import jax.numpy as jnp
from jax import lax
from jax.experimental import pallas as pl
from jax.experimental.pallas import tpu as pltpu
from jax.sharding import PartitionSpec as P

D = 768
HEADS = 12
FF = 3072
SD = 128
PH = 2
NCLS = 14
BLK = 128
STEP = 10
NBLK = 439
TILE = 512
PAIRS = 3
GROUPS = 2
CHUNK = 1024
LATE = 24

NORM_EPSILON = 1e-12
BETA_ONE = 0.9
BETA_TWO = 0.999
ADAM_EPSILON = 1e-08
ADAM_RATE = 0.1
MATRIX_RATE = 0.2
STAT_DECAY = 0.5
MASKED_SCORE = -1e30
HIGHEST_PRECISION = lax.Precision.HIGHEST
MIB = 1024 * 1024
F32 = jnp.float32
BF16 = jnp.bfloat16

def product(former, latter, precision=None):
    return jnp.dot(former, latter, preferred_element_type=F32, precision=precision)


def left_product(former, latter, precision=None):
    return lax.dot_general(
        former, latter, (((0,), (0,)), ((), ())), preferred_element_type=F32, precision=precision
    )


def right_product(former, latter, precision=None):
    return lax.dot_general(
        former, latter, (((1,), (1,)), ((), ())), preferred_element_type=F32, precision=precision
    )


def unpack(small_values):
    widths = (D, D, D, D, D, FF, D, D, D, SD, SD, SD, SD * NCLS, NCLS)
    pieces = []
    offset = 0
    for column_count in widths:
        pieces.append(small_values[offset : offset + column_count])
        offset += column_count
    return pieces


def each_block(first, row_count, col_count, action):
    def one_row(index, carry):
        row = pl.multiple_of(index * BLK, BLK)
        for col in range(col_count):
            action(first + index * col_count + col, row, col * BLK)
        return carry

    lax.fori_loop(0, row_count, one_row, 0)


def load_blocks(slot_ref, blocks, target, sem, first, row_count, col_count, col_start=0):
    def move(block, row, col):
        pltpu.make_async_copy(
            blocks.at[slot_ref[block]],
            target.at[pl.ds(row, BLK), pl.ds(col + col_start * BLK, BLK)],
            sem,
        ).start()

    each_block(first, row_count, col_count, move)


def wait_whole(target, sem):
    pltpu.make_async_copy(target, target, sem).wait()


def assemble_kernel(slot_ref, blocks, out, sem):
    for which in range(3):
        load_blocks(slot_ref, blocks, out, sem, 36 * which, 6, 6, 6 * which)
    wait_whole(out, sem)


def assemble(block_slot, blocks):
    return pl.pallas_call(
        assemble_kernel,
        grid_spec=pltpu.PrefetchScalarGridSpec(
            num_scalar_prefetch=1,
            grid=(1,),
            in_specs=[pl.BlockSpec(memory_space=pltpu.HBM)],
            out_specs=pl.BlockSpec(memory_space=pltpu.VMEM),
            scratch_shapes=[pltpu.SemaphoreType.DMA],
        ),
        out_shape=jax.ShapeDtypeStruct((D, 3 * D), BF16),
        compiler_params=pltpu.CompilerParams(vmem_limit_bytes=60 * MIB),
        name="assemble",
    )(block_slot, blocks)


def join_small(small_ref, query_ref, value_ref, small_out):
    small_out[...] = small_ref[...]
    for start, ref in ((0, query_ref), (D // BLK, value_ref)):
        for index in range(D // BLK):
            small_out[start + index : start + index + 1, :] = ref[:, index * BLK : (index + 1) * BLK]


PART = 512
ACROSS = PART // BLK


def feed_grads_kernel(
    code_ref,
    first_turned,
    down_turned,
    active_ref,
    d_up_ref,
    g_out,
    g_student,
    g_hidden,
    terms,
    up_stage,
    down_stage,
    up_sems,
    down_sems,
    other_sems,
):
    step = pl.program_id(0)
    last = pl.num_programs(0) - 1
    slot = step % 2
    others = ((g_out, 108, 6, 6), (g_student, 432, 6, 1), (g_hidden, 438, 1, 1))

    @pl.when(step == 0)
    def _():
        for which, (grad, first, row_count, col_count) in enumerate(others):

            def move(block, row, col, which=which, grad=grad):
                pltpu.make_async_copy(
                    grad.at[pl.ds(row, BLK), pl.ds(col, BLK)], terms.at[code_ref[block]], other_sems.at[which]
                ).start()

            each_block(first, row_count, col_count, move)

    @pl.when(step >= 2)
    def _():
        wait_whole(up_stage.at[slot], up_sems.at[slot])
        wait_whole(down_stage.at[slot], down_sems.at[slot])

    up_stage[slot] = product(first_turned[...], d_up_ref[...]).astype(BF16)
    down_stage[slot] = product(down_turned[...], active_ref[...]).T.astype(BF16)
    for row in range(D // BLK):
        for col in range(ACROSS):
            pltpu.make_async_copy(
                up_stage.at[slot, pl.ds(row * BLK, BLK), pl.ds(col * BLK, BLK)],
                terms.at[code_ref[144 + row * (FF // BLK) + step * ACROSS + col]],
                up_sems.at[slot],
            ).start()
            pltpu.make_async_copy(
                down_stage.at[slot, pl.ds(col * BLK, BLK), pl.ds(row * BLK, BLK)],
                terms.at[code_ref[288 + (step * ACROSS + col) * (D // BLK) + row]],
                down_sems.at[slot],
            ).start()

    @pl.when(step == last)
    def _():
        for place in range(2):
            wait_whole(up_stage.at[place], up_sems.at[place])
            wait_whole(down_stage.at[place], down_sems.at[place])
        for which, (grad, *_) in enumerate(others):
            wait_whole(grad, other_sems.at[which])


def feed_grads(code, first, d_down, active, d_up, others, slot_count):
    tokens = first.shape[1]

    def whole(shape):
        return pl.BlockSpec(shape, lambda step, *_: (0, 0), pipeline_mode=pl.Buffered(1))

    part = pl.BlockSpec((tokens, PART), lambda step, *_: (0, step))
    return pl.pallas_call(
        feed_grads_kernel,
        grid_spec=pltpu.PrefetchScalarGridSpec(
            num_scalar_prefetch=1,
            grid=(FF // PART,),
            in_specs=[whole(first.shape), whole(d_down.shape), part, part]
            + [whole(other.shape) for other in others],
            out_specs=pl.BlockSpec(memory_space=pltpu.HBM),
            scratch_shapes=[
                pltpu.VMEM((2, D, PART), BF16),
                pltpu.VMEM((2, PART, D), BF16),
                pltpu.SemaphoreType.DMA((2,)),
                pltpu.SemaphoreType.DMA((2,)),
                pltpu.SemaphoreType.DMA((3,)),
            ],
        ),
        out_shape=jax.ShapeDtypeStruct((slot_count, BLK, BLK), BF16),
        compiler_params=pltpu.CompilerParams(vmem_limit_bytes=60 * MIB),
        cost_estimate=pl.CostEstimate(
            flops=4 * tokens * D * FF, bytes_accessed=50 * MIB, transcendentals=0
        ),
        name="feed_grads",
    )(code, first, d_down, active, d_up, *others)


def input_weights_kernel(
    code_ref, turned, d_ref, small_ref, query_ref, value_ref, _, terms, small_out, stage, sems
):
    step = pl.program_id(0)
    slot = step % 2

    @pl.when(step == 0)
    def _():
        join_small(small_ref, query_ref, value_ref, small_out)

    @pl.when(step >= 2)
    def _():
        wait_whole(stage.at[slot], sems.at[slot])

    stage[slot] = product(turned[...], d_ref[...]).astype(BF16)
    for row in range(D // BLK):
        for col in range(D // BLK):
            pltpu.make_async_copy(
                stage.at[slot, pl.ds(row * BLK, BLK), pl.ds(col * BLK, BLK)],
                terms.at[code_ref[36 * step + row * (D // BLK) + col]],
                sems.at[slot],
            ).start()

    @pl.when(step == pl.num_programs(0) - 1)
    def _():
        for place in range(2):
            wait_whole(stage.at[place], sems.at[place])


def input_weights(code, x, d_qkv, small, g_query, g_value, terms):
    tokens = x.shape[1]

    def whole(shape):
        return pl.BlockSpec(shape, lambda step, *_: (0, 0), pipeline_mode=pl.Buffered(1))

    hbm = pl.BlockSpec(memory_space=pltpu.HBM)
    return pl.pallas_call(
        input_weights_kernel,
        grid_spec=pltpu.PrefetchScalarGridSpec(
            num_scalar_prefetch=1,
            grid=(3,),
            in_specs=[
                whole(x.shape),
                pl.BlockSpec((tokens, D), lambda step, *_: (0, step)),
                whole(small.shape),
                whole(g_query.shape),
                whole(g_value.shape),
                hbm,
            ],
            out_specs=[hbm, pl.BlockSpec(small.shape, lambda step, *_: (0, 0))],
            scratch_shapes=[
                pltpu.VMEM((2, D, D), BF16),
                pltpu.SemaphoreType.DMA((2,)),
            ],
        ),
        out_shape=[
            jax.ShapeDtypeStruct(terms.shape, BF16),
            jax.ShapeDtypeStruct(small.shape, F32),
        ],
        input_output_aliases={6: 0},
        compiler_params=pltpu.CompilerParams(vmem_limit_bytes=60 * MIB),
        cost_estimate=pl.CostEstimate(
            flops=6 * tokens * D * D, bytes_accessed=16 * MIB, transcendentals=0
        ),
        name="input_weights",
    )(code, x, d_qkv, small, g_query, g_value, terms)


def half_masks():
    lane = lax.broadcasted_iota(jnp.int32, (1, BLK), 1)
    low = (lane < BLK // 2).astype(BF16)
    return low, (1.0 - low.astype(F32)).astype(BF16)


def stack_heads(values, low, high):
    return jnp.concatenate([values * low, values * high], axis=0)


def pick_heads(values):
    rows = values.shape[0] // 2
    lane = lax.broadcasted_iota(jnp.int32, (rows, BLK), 1)
    return jnp.where(lane < BLK // 2, values[:rows], values[rows:])


def pipelined(count, before, middle, after):
    started = before(0)
    done = None
    for index in range(count):
        current = started
        if index + 1 < count:
            started = before(index + 1)
        if done is not None:
            after(index - 1, done)
        done = middle(index, current)
    after(count - 1, done)


def softmax(scores, length):
    visible = lax.broadcasted_iota(jnp.int32, scores.shape, 1) < length
    scores = jnp.where(visible, scores, MASKED_SCORE)
    powers = jnp.exp(scores - jnp.max(scores, axis=-1, keepdims=True))
    total = jnp.sum(powers, axis=-1, keepdims=True)
    return (powers * (1.0 / total)).astype(BF16)


def attention_kernel(
    len_short,
    len_long,
    x_short_ref,
    x_long_ref,
    params,
    w_ref,
    x_ref,
    q_ref,
    k_ref,
    v_ref,
    context_ref,
    short_ref,
    long_ref,
    bias,
    *,
    short_tiles,
):
    tile = pl.program_id(0)
    group = pl.program_id(1)
    low, high = half_masks()
    width = short_ref.shape[-1]
    per_tile = TILE // width

    wide = PAIRS * BLK
    start = pl.multiple_of(group * wide, wide)

    @pl.when((tile == 0) & (group == 0))
    def _():
        for which in range(2):
            for place in range(D // BLK):
                row = which * (D // BLK) + place
                bias[which : which + 1, place * BLK : (place + 1) * BLK] = params[row : row + 1, :]

    @pl.when((tile < short_tiles) & (group == 0))
    def _():
        x_ref[...] = x_short_ref[...]

    @pl.when((tile >= short_tiles) & (group == 0))
    def _():
        x_ref[...] = x_long_ref[...]

    @pl.when(group == 0)
    def _():
        rows_in = x_ref[...]
        queries = product(rows_in, w_ref[:, :D]) + bias[0:1, :]
        q_ref[...] = (queries * 0.125).astype(BF16)
        k_ref[...] = product(rows_in, w_ref[:, D : 2 * D]).astype(BF16)
        v_ref[...] = (product(rows_in, w_ref[:, 2 * D :]) + bias[1:2, :]).astype(BF16)

    def inner(pair):
        return pl.ds(pl.multiple_of(start + pair * BLK, BLK), BLK)

    def attend(units, kept_ref):
        def scores(index):
            rows, keys, pair, _, _ = units[index]
            return right_product(stack_heads(q_ref[rows, inner(pair)], low, high), k_ref[keys, inner(pair)])

        def weigh(index, values):
            _, _, _, length, place = units[index]
            probs = softmax(values, length)
            kept_ref[place] = probs
            return probs

        def mix(index, probs):
            rows, keys, pair, _, _ = units[index]
            mixed = pick_heads(product(probs, v_ref[keys, inner(pair)])).astype(BF16)
            context_ref[rows, pair * BLK : (pair + 1) * BLK] = mixed

        pipelined(len(units), scores, weigh, mix)

    @pl.when(tile < short_tiles)
    def _():
        units = []
        for seq in range(per_tile):
            rows = slice(seq * width, (seq + 1) * width)
            length = len_short[tile * per_tile + seq]
            for pair in range(PAIRS):
                units.append((rows, rows, pair, length, (0, pair, seq)))
        attend(units, short_ref)

    @pl.when(tile >= short_tiles)
    def _():
        length = len_long[tile - short_tiles]
        half = TILE // 2
        units = []
        for pair in range(PAIRS):
            for part in range(2):
                rows = slice(part * half, (part + 1) * half)
                units.append((rows, slice(0, TILE), pair, length, (0, pair, part)))
        attend(units, long_ref)


def run_events(step, events):
    for index, actions in enumerate(events):

        @pl.when(step == index)
        def _(actions=actions):
            for action in actions:
                action()


def probs_shapes(short_tiles, long_tiles, width):
    per_tile = TILE // width
    return (
        (short_tiles, 2 * PAIRS, per_tile, 2 * width, width),
        (long_tiles, 2 * PAIRS, 2, TILE, TILE),
    )


def short_index(tile, short_tiles):
    return jnp.minimum(tile, short_tiles - 1)


def long_index(tile, short_tiles):
    return jnp.maximum(tile - short_tiles, 0)


def probs_maps(short_tiles):
    def short_map(tile, group):
        last = jnp.minimum(tile // short_tiles, 1)
        return (short_index(tile, short_tiles), group + last * (GROUPS - 1 - group), 0, 0, 0)

    def long_map(tile, group):
        begun = jnp.minimum(tile // short_tiles, 1)
        return (long_index(tile, short_tiles), begun * group, 0, 0, 0)

    return short_map, long_map


def attention(len_short, len_long, x_short, x_long, params, w_qkv, short_tiles, width):
    tiles = (x_short.shape[0] + x_long.shape[0]) // TILE
    wide = PAIRS * BLK
    short_shape, long_shape = probs_shapes(short_tiles, tiles - short_tiles, width)
    short_map, long_map = probs_maps(short_tiles)
    flops = 4 * D * TILE * TILE * tiles + 6 * D * D * TILE * tiles
    rows = pl.BlockSpec((TILE, wide), lambda tile, group: (tile, group))
    scalars = pl.BlockSpec(memory_space=pltpu.SMEM)

    def whole(shape):
        return pl.BlockSpec(shape, lambda tile, group: (0,) * len(shape), pipeline_mode=pl.Buffered(1))

    in_specs = [
        scalars,
        scalars,
        pl.BlockSpec((TILE, D), lambda tile, group: (short_index(tile, short_tiles), 0)),
        pl.BlockSpec((TILE, D), lambda tile, group: (long_index(tile, short_tiles), 0)),
        whole(params.shape),
        whole((D, 3 * D)),
    ]
    full_rows = pl.BlockSpec((TILE, D), lambda tile, group: (tile, 0))
    out_specs = [
        full_rows,
        full_rows,
        full_rows,
        full_rows,
        rows,
        pl.BlockSpec((1, PAIRS) + short_shape[2:], short_map),
        pl.BlockSpec((1, PAIRS) + long_shape[2:], long_map),
    ]
    out_shape = [jax.ShapeDtypeStruct((tiles * TILE, D), BF16)] * 5 + [
        jax.ShapeDtypeStruct(short_shape, BF16),
        jax.ShapeDtypeStruct(long_shape, BF16),
    ]
    arguments = [len_short, len_long, x_short, x_long, params, w_qkv]
    return pl.pallas_call(
        partial(attention_kernel, short_tiles=short_tiles),
        grid=(tiles, GROUPS),
        in_specs=in_specs,
        out_specs=out_specs,
        out_shape=out_shape,
        scratch_shapes=[pltpu.VMEM((8, D), F32)],
        compiler_params=pltpu.CompilerParams(vmem_limit_bytes=60 * MIB),
        cost_estimate=pl.CostEstimate(
            flops=flops, bytes_accessed=35 * MIB, transcendentals=HEADS * TILE * TILE * tiles // 2
        ),
        name="attention",
    )(*arguments)


def attention_back_kernel(*refs, short_tiles, transfers):
    q_ref, k_ref, v_ref, short_ref, long_ref, dc_ref, x_ref = refs[:7]
    refs = refs[7:]
    if transfers:
        terms_ref, refs = refs[0], refs[1:]
    out_ref, bq_ref, bv_ref, turned_ref = refs[:4]
    tile = pl.program_id(0)
    group = pl.program_id(1)
    low, high = half_masks()
    width = short_ref.shape[-1]
    per_tile = TILE // width
    if transfers:
        reduce = Reduce(terms_ref, 0, refs[4], refs[5:])
        run_events(
            tile * GROUPS + group,
            (
                (reduce.start,),
                (partial(reduce.core, 0),),
                (partial(reduce.core, 1), partial(reduce.first, 0)),
                (partial(reduce.core, 2), partial(reduce.first, 1), partial(reduce.second, 0)),
                (partial(reduce.core, 3), partial(reduce.first, 2), partial(reduce.second, 1)),
                (partial(reduce.first, 3), partial(reduce.second, 2)),
                (partial(reduce.second, 3), reduce.share),
                (reduce.share_on,),
            ),
        )

    wide = PAIRS * BLK
    start = pl.multiple_of(group * wide, wide)

    def columns(which, cols):
        return pl.ds(pl.multiple_of(which * D + start + cols.start, BLK), BLK)

    def go_back(units, kept_ref, parts):
        sums = {}

        def spread_in(index):
            rows, keys, cols, _ = units[index]
            return right_product(stack_heads(dc_ref[rows, cols], low, high), v_ref[keys, cols])

        def differ(index, d_probs):
            wide = kept_ref[units[index][3]].astype(F32)
            weighted = wide * d_probs
            return (weighted - wide * jnp.sum(weighted, axis=-1, keepdims=True)).astype(BF16)

        def gather_up(index, d_scores):
            rows, keys, cols, place = units[index]
            d_queries = pick_heads(product(d_scores, k_ref[keys, cols])) * 0.125
            out_ref[rows, columns(0, cols)] = d_queries.astype(BF16)
            d_keys = left_product(d_scores, stack_heads(q_ref[rows, cols], low, high))
            d_values = left_product(kept_ref[place], stack_heads(dc_ref[rows, cols], low, high))
            if index % parts:
                d_keys += sums["keys"]
                d_values += sums["values"]
            if index % parts == parts - 1:
                out_ref[keys, columns(1, cols)] = d_keys.astype(BF16)
                out_ref[keys, columns(2, cols)] = d_values.astype(BF16)
            else:
                sums.update(keys=d_keys, values=d_values)

        pipelined(len(units), spread_in, differ, gather_up)

    @pl.when(tile < short_tiles)
    def _():
        units = []
        for seq in range(per_tile):
            rows = slice(seq * width, (seq + 1) * width)
            for pair in range(PAIRS):
                cols = slice(pair * BLK, (pair + 1) * BLK)
                units.append((rows, rows, cols, (0, pair, seq)))
        go_back(units, short_ref, 1)

    @pl.when(tile >= short_tiles)
    def _():
        half = TILE // 2
        units = []
        for pair in range(PAIRS):
            cols = slice(pair * BLK, (pair + 1) * BLK)
            for part in range(2):
                rows = slice(part * half, (part + 1) * half)
                units.append((rows, slice(0, TILE), cols, (0, pair, part)))
        go_back(units, long_ref, 2)

    @pl.when(group == 0)
    def _():
        turned_ref[...] = x_ref[...].T

    @pl.when((tile == 0) & (group == 0))
    def _():
        bq_ref[...] = jnp.zeros_like(bq_ref)
        bv_ref[...] = jnp.zeros_like(bv_ref)

    bq_ref[:, pl.ds(start, wide)] += column_sum(out_ref[:, pl.ds(start, wide)])
    bv_ref[:, pl.ds(start, wide)] += column_sum(out_ref[:, pl.ds(2 * D + start, wide)])

    if transfers:

        @pl.when((tile == pl.num_programs(0) - 1) & (group == GROUPS - 1))
        def _():
            reduce.finish()


def attention_back(qkv, probs_short, probs_long, d_context, x, short_tiles, terms=None, count=0):
    tiles = d_context.shape[0] // TILE
    wide = PAIRS * BLK
    short_map, long_map = probs_maps(short_tiles)
    rows = pl.BlockSpec((TILE, wide), lambda tile, group: (tile, group))
    row = pl.BlockSpec((1, D), lambda tile, group: (0, 0))
    flops = 10 * D * TILE * TILE * tiles
    in_specs = [
        rows,
        rows,
        rows,
        pl.BlockSpec((1, PAIRS) + probs_short.shape[2:], short_map),
        pl.BlockSpec((1, PAIRS) + probs_long.shape[2:], long_map),
        rows,
        pl.BlockSpec((TILE, D), lambda tile, group: (tile, 0)),
    ]
    out_specs = [
        pl.BlockSpec((TILE, 3 * D), lambda tile, group: (tile, 0)),
        row,
        row,
        pl.BlockSpec((D, TILE), lambda tile, group: (0, tile)),
    ]
    out_shape = [
        jax.ShapeDtypeStruct((tiles * TILE, 3 * D), BF16),
        jax.ShapeDtypeStruct((1, D), F32),
        jax.ShapeDtypeStruct((1, D), F32),
        jax.ShapeDtypeStruct((D, tiles * TILE), BF16),
    ]
    arguments = [*qkv, probs_short, probs_long, d_context, x]
    scratch = []
    params = dict(vmem_limit_bytes=60 * MIB)
    if terms is not None:
        arguments.append(terms)
        in_specs.append(pl.BlockSpec(memory_space=pltpu.HBM))
        out_specs.append(pl.BlockSpec((count, BLK), lambda tile, group: (0, 0)))
        out_shape.append(jax.ShapeDtypeStruct((count, BLK), BF16))
        scratch = reduce_scratch(count)
        params.update(collective_id=2, has_side_effects=True)
    return pl.pallas_call(
        partial(attention_back_kernel, short_tiles=short_tiles, transfers=terms is not None),
        grid=(tiles, GROUPS),
        in_specs=in_specs,
        out_specs=out_specs,
        out_shape=out_shape,
        scratch_shapes=scratch,
        compiler_params=pltpu.CompilerParams(**params),
        cost_estimate=pl.CostEstimate(flops=flops, bytes_accessed=50 * MIB, transcendentals=0),
        name="attention_back",
    )(*arguments)


INPUT_ROWS = 256


def input_product(d_ref, resid_ref, w_ref, short_ref, long_ref, short_steps):
    step = pl.program_id(0)
    total = resid_ref[...] + right_product(d_ref[...], w_ref[...])

    @pl.when(step < short_steps)
    def _():
        short_ref[...] = total

    @pl.when(step >= short_steps)
    def _():
        long_ref[...] = total


def input_specs(short_steps):
    rows = [pl.BlockSpec((INPUT_ROWS, width), lambda step: (step, 0)) for width in (3 * D, D)]
    whole = pl.BlockSpec((D, 3 * D), lambda step: (0, 0), pipeline_mode=pl.Buffered(1))
    outs = [
        pl.BlockSpec((INPUT_ROWS, D), lambda step: (short_index(step, short_steps), 0)),
        pl.BlockSpec((INPUT_ROWS, D), lambda step: (long_index(step, short_steps), 0)),
    ]
    return rows + [whole], outs


def input_grads(d_qkv, resid, w_qkv, short_tiles):
    steps = resid.shape[0] // INPUT_ROWS
    short_steps = short_tiles * TILE // INPUT_ROWS
    in_specs, out_specs = input_specs(short_steps)
    return pl.pallas_call(
        partial(input_product, short_steps=short_steps),
        grid=(steps,),
        in_specs=in_specs,
        out_specs=out_specs,
        out_shape=[
            jax.ShapeDtypeStruct((short_steps * INPUT_ROWS, D), F32),
            jax.ShapeDtypeStruct(((steps - short_steps) * INPUT_ROWS, D), F32),
        ],
        compiler_params=pltpu.CompilerParams(vmem_limit_bytes=60 * MIB),
        name="input_grads",
    )(d_qkv, resid, w_qkv)


def normal_parts(values):
    below = 0.5 * lax.erf(values * 0.7071067811865476) + 0.5
    return below, jnp.exp(-0.5 * values * values) * 0.3989422804014327


B_OUT, GAIN_ONE, SHIFT_ONE, B_UP, B_DOWN, GAIN_TWO, SHIFT_TWO, B_STUDENT, POOL_QUERY, B_HIDDEN = range(10)
VECTORS = (
    (12, 6),
    (18, 6),
    (24, 6),
    (30, 24),
    (54, 6),
    (60, 6),
    (66, 6),
    (72, 1),
    (73, 1),
    (74, 1),
)
CLASS_ROW = 75
LAST_ROW = 91
SMALL_ROWS = 96


def norm_parts(values):
    center = values - jnp.mean(values, axis=-1, keepdims=True)
    spread = jnp.mean(center * center, axis=-1, keepdims=True)
    inverse = lax.rsqrt(spread + NORM_EPSILON)
    return center * inverse, inverse


def norm_back(d_values, gain, unit, inverse):
    d_unit = d_values * gain
    return inverse * (
        d_unit
        - jnp.mean(d_unit, axis=-1, keepdims=True)
        - unit * jnp.mean(d_unit * unit, axis=-1, keepdims=True)
    )


def column_sum(values):
    return jnp.sum(values.astype(F32), axis=0, keepdims=True)


def pool_weights(student, query, length):
    scaled = student * query
    lane = lax.broadcasted_iota(jnp.int32, scaled.shape, 1)
    place = lax.broadcasted_iota(jnp.int32, (scaled.shape[0], 1), 0)
    weights = []
    for side in (lane < SD // PH, lane >= SD // PH):
        scores = jnp.sum(jnp.where(side, scaled, 0.0), axis=-1, keepdims=True)
        scores = jnp.where(place < length, scores, MASKED_SCORE)
        powers = jnp.exp(scores - jnp.max(scores, axis=0, keepdims=True))
        weights.append(powers / jnp.sum(powers, axis=0, keepdims=True))
    return jnp.where(lane < SD // PH, weights[0], weights[1]), weights


def student_back(student, query, weights, both, d_pooled):
    lane = lax.broadcasted_iota(jnp.int32, student.shape, 1)
    moved = student * d_pooled
    d_scores = []
    for side, weight in zip((lane < SD // PH, lane >= SD // PH), weights):
        d_weight = jnp.sum(jnp.where(side, moved, 0.0), axis=-1, keepdims=True)
        d_scores.append(weight * (d_weight - jnp.sum(weight * d_weight, axis=0, keepdims=True)))
    d_score = jnp.where(lane < SD // PH, d_scores[0], d_scores[1])
    d_query = jnp.sum(d_score * student, axis=0, keepdims=True) * 0.125
    return both * d_pooled + d_score * query, d_query


def feed_kernel(
    len_short,
    len_long,
    slot_ref,
    x_ref,
    context_ref,
    cot_short_ref,
    cot_long_ref,
    logit_cot_short,
    logit_cot_long,
    params,
    w_class_ref,
    b_class_ref,
    blocks,
    enc_short_ref,
    enc_long_ref,
    logits_short,
    logits_long,
    first_ref,
    active_ref,
    d_up_ref,
    d_down_ref,
    d_branch_ref,
    d_context_ref,
    d_resid_ref,
    g_student,
    g_hidden,
    g_small,
    slope,
    pooled_ref,
    d_student_ref,
    w_out,
    w_up,
    w_down,
    w_student,
    w_hidden,
    vectors,
    totals,
    g_class,
    g_last,
    w_class,
    b_class,
    logit_cot,
    sems,
    *,
    short_tiles,
    width,
):
    tile = pl.program_id(0)
    per_tile = TILE // width
    loads = ((w_out, 108, 6, 6), (w_up, 144, 6, 24), (w_down, 288, 24, 6), (w_student, 432, 6, 1), (w_hidden, 438, 1, 1))

    def arrive(*indices):
        @pl.when(tile == 0)
        def _():
            for index in indices:
                wait_whole(loads[index][0], sems.at[index])

    @pl.when(tile == 0)
    def _():
        for index, (target, block, row_count, col_count) in enumerate(loads):
            load_blocks(slot_ref, blocks, target, sems.at[index], block, row_count, col_count)
        for index, (start, count) in enumerate(VECTORS):
            for place in range(count):
                vectors[index : index + 1, place * BLK : (place + 1) * BLK] = params[
                    start + place : start + place + 1, :
                ]
        for ref in (totals, g_class, g_last, g_student, g_hidden, w_class, b_class):
            ref[...] = jnp.zeros_like(ref)
        w_class[:, :NCLS] = w_class_ref[...]
        b_class[:, :NCLS] = b_class_ref[...]

    def vector(index):
        return vectors[index : index + 1, : VECTORS[index][1] * BLK]

    def add_total(index, values):
        totals[index : index + 1, : VECTORS[index][1] * BLK] += column_sum(values)

    arrive(0)
    branch = product(context_ref[...], w_out[...]) + vector(B_OUT)
    unit_one, inverse_one = norm_parts(x_ref[...].astype(F32) + branch)
    first = (unit_one * vector(GAIN_ONE) + vector(SHIFT_ONE)).astype(BF16)
    first_ref[...] = first.T
    arrive(1)
    chunks = [slice(start, start + CHUNK) for start in range(0, FF, CHUNK)]

    def rise(index):
        return product(first, w_up[:, chunks[index]])

    def bend(index, upward):
        upward = upward + vectors[B_UP : B_UP + 1, chunks[index]]
        below, density = normal_parts(upward)
        active_ref[:, chunks[index]] = (upward * below).astype(BF16)
        slope[:, chunks[index]] = (below + upward * density).astype(BF16)

    pipelined(len(chunks), rise, bend, lambda *_: None)
    arrive(2, 3, 4)
    downward = product(active_ref[...], w_down[...]) + vector(B_DOWN)
    unit_two, inverse_two = norm_parts(first.astype(F32) + downward)
    encoded = (unit_two * vector(GAIN_TWO) + vector(SHIFT_TWO)).astype(BF16)

    @pl.when(tile < short_tiles)
    def _():
        enc_short_ref[...] = encoded

    @pl.when(tile >= short_tiles)
    def _():
        enc_long_ref[...] = encoded

    student = product(encoded, w_student[...]) + vector(B_STUDENT)
    query = vector(POOL_QUERY) * 0.125
    pooled_ref[...] = jnp.zeros_like(pooled_ref)

    def head():
        pooled = pooled_ref[...]
        wide_hidden = w_hidden[...].astype(F32)
        hidden = jnp.tanh(product(pooled, wide_hidden, HIGHEST_PRECISION) + vector(B_HIDDEN))
        logits = product(hidden, w_class[...], HIGHEST_PRECISION) + b_class[...]
        d_logits = logit_cot[...]
        g_last[...] += column_sum(d_logits)
        g_class[...] += left_product(d_logits, hidden, HIGHEST_PRECISION)
        d_hidden = right_product(d_logits, w_class[...], HIGHEST_PRECISION)
        d_hidden = d_hidden * (1.0 - hidden * hidden)
        add_total(B_HIDDEN, d_hidden)
        g_hidden[...] += left_product(pooled, d_hidden, HIGHEST_PRECISION)
        return logits, right_product(d_hidden, wide_hidden, HIGHEST_PRECISION)

    def pool(starts, size, lengths, cot_ref, logits_ref, first):
        count = len(starts)
        logit_cot[...] = jnp.zeros_like(logit_cot)
        for index in range(count):
            logit_cot[index : index + 1, :NCLS] = cot_ref[pl.ds(first + index, 1), :]
        kept = []
        for index, (start, length) in enumerate(zip(starts, lengths)):
            rows = student[start : start + size]
            both, weights = pool_weights(rows, query, length)
            pooled_ref[index : index + 1, :] = column_sum(both * rows)
            kept.append((start, rows, both, weights))
        logits, d_pooled = head()
        for index in range(count):
            logits_ref[pl.ds(first + index, 1), :] = logits[index : index + 1, :NCLS]
        for index, (start, rows, both, weights) in enumerate(kept):
            d_rows, d_query = student_back(rows, query, weights, both, d_pooled[index : index + 1])
            d_student_ref[start : start + size, :] = d_rows.astype(BF16)
            add_total(POOL_QUERY, d_query)

    @pl.when(tile < short_tiles)
    def _():
        pool(
            [seq * width for seq in range(per_tile)],
            width,
            [len_short[tile * per_tile + seq] for seq in range(per_tile)],
            logit_cot_short,
            logits_short,
            tile * per_tile,
        )

    @pl.when(tile >= short_tiles)
    def _():
        long = tile - short_tiles
        pool([0], TILE, [len_long[long]], logit_cot_long, logits_long, long)

    d_student = d_student_ref[...]
    add_total(B_STUDENT, d_student)
    g_student[...] += left_product(encoded, d_student)
    cotangent = jnp.where(tile < short_tiles, cot_short_ref[...], cot_long_ref[...])
    d_second = cotangent.astype(F32) + right_product(d_student, w_student[...])
    add_total(GAIN_TWO, d_second * unit_two)
    add_total(SHIFT_TWO, d_second)
    d_resid_two = norm_back(d_second, vector(GAIN_TWO), unit_two, inverse_two)
    d_down = d_resid_two.astype(BF16)
    d_down_ref[...] = d_down.T
    add_total(B_DOWN, d_down)

    def fall(index):
        return right_product(d_down, w_down[chunks[index], :])

    def bend_back(index, d_active):
        d_up = (d_active * slope[:, chunks[index]].astype(F32)).astype(BF16)
        d_up_ref[:, chunks[index]] = d_up
        totals[B_UP : B_UP + 1, chunks[index]] += column_sum(d_up)

    pipelined(len(chunks), fall, bend_back, lambda *_: None)
    d_first = d_resid_two + right_product(d_up_ref[...], w_up[...])
    add_total(GAIN_ONE, d_first * unit_one)
    add_total(SHIFT_ONE, d_first)
    d_resid_one = norm_back(d_first, vector(GAIN_ONE), unit_one, inverse_one)
    d_resid_ref[...] = d_resid_one
    d_branch = d_resid_one.astype(BF16)
    d_branch_ref[...] = d_branch
    add_total(B_OUT, d_branch)
    d_context_ref[...] = right_product(d_branch, w_out[...]).astype(BF16)

    @pl.when(tile == pl.num_programs(0) - 1)
    def _():
        g_small[...] = jnp.zeros_like(g_small)
        for index, (start, count) in enumerate(VECTORS):
            for place in range(count):
                g_small[start + place : start + place + 1, :] = totals[
                    index : index + 1, place * BLK : (place + 1) * BLK
                ]
        g_small[CLASS_ROW : CLASS_ROW + NCLS, :] = g_class[:NCLS, :]
        g_small[LAST_ROW : LAST_ROW + 1, :] = g_last[...]


def feed(
    len_short, len_long, block_slot, x, context, cot_short, cot_long, logit_cots, small, blocks, short_tiles, width
):
    tiles = x.shape[0] // TILE
    long_tiles = tiles - short_tiles

    def whole(shape):
        return pl.BlockSpec(shape, lambda tile, *_: (0,) * len(shape), pipeline_mode=pl.Buffered(1))

    def kept(shape):
        return pl.BlockSpec(shape, lambda tile, *_: (0,) * len(shape))

    def rows(columns):
        return pl.BlockSpec((TILE, columns), lambda tile, *_: (tile, 0))

    turned = pl.BlockSpec((D, TILE), lambda tile, *_: (0, tile))
    short_rows = pl.BlockSpec((TILE, D), lambda tile, *_: (short_index(tile, short_tiles), 0))
    long_rows = pl.BlockSpec((TILE, D), lambda tile, *_: (long_index(tile, short_tiles), 0))
    grad_shapes = ((D, SD), (SD, SD), (SMALL_ROWS, BLK))
    total = tiles * TILE
    return pl.pallas_call(
        partial(feed_kernel, short_tiles=short_tiles, width=width),
        grid_spec=pltpu.PrefetchScalarGridSpec(
            num_scalar_prefetch=3,
            grid=(tiles,),
            in_specs=[rows(D), rows(D), short_rows, long_rows]
            + [whole(array.shape) for array in (*logit_cots, *small)]
            + [pl.BlockSpec(memory_space=pltpu.HBM)],
            out_specs=[
                short_rows,
                long_rows,
                kept(logit_cots[0].shape),
                kept(logit_cots[1].shape),
                turned,
                rows(FF),
                rows(FF),
                turned,
                rows(D),
                rows(D),
                rows(D),
            ]
            + [kept(shape) for shape in grad_shapes],
            scratch_shapes=[
                pltpu.VMEM((TILE, FF), BF16),
                pltpu.VMEM((8, SD), F32),
                pltpu.VMEM((TILE, SD), BF16),
                pltpu.VMEM((D, D), BF16),
                pltpu.VMEM((D, FF), BF16),
                pltpu.VMEM((FF, D), BF16),
                pltpu.VMEM((D, SD), BF16),
                pltpu.VMEM((SD, SD), BF16),
                pltpu.VMEM((16, FF), F32),
                pltpu.VMEM((16, FF), F32),
                pltpu.VMEM((SD, SD), F32),
                pltpu.VMEM((1, SD), F32),
                pltpu.VMEM((SD, SD), F32),
                pltpu.VMEM((1, SD), F32),
                pltpu.VMEM((8, SD), F32),
                pltpu.SemaphoreType.DMA((5,)),
            ],
        ),
        out_shape=[
            jax.ShapeDtypeStruct((short_tiles * TILE, D), BF16),
            jax.ShapeDtypeStruct((long_tiles * TILE, D), BF16),
            jax.ShapeDtypeStruct(logit_cots[0].shape, F32),
            jax.ShapeDtypeStruct(logit_cots[1].shape, F32),
            jax.ShapeDtypeStruct((D, total), BF16),
            jax.ShapeDtypeStruct((total, FF), BF16),
            jax.ShapeDtypeStruct((total, FF), BF16),
            jax.ShapeDtypeStruct((D, total), BF16),
            jax.ShapeDtypeStruct((total, D), BF16),
            jax.ShapeDtypeStruct((total, D), BF16),
            jax.ShapeDtypeStruct((total, D), F32),
        ]
        + [jax.ShapeDtypeStruct(shape, F32) for shape in grad_shapes],
        compiler_params=pltpu.CompilerParams(vmem_limit_bytes=62 * MIB),
        cost_estimate=pl.CostEstimate(
            flops=total * (8 * D * FF + 4 * D * D), bytes_accessed=70 * MIB, transcendentals=total * FF
        ),
        name="feed",
    )(len_short, len_long, block_slot, x, context, cot_short, cot_long, *logit_cots, *small, blocks)


class Place:
    def __init__(self):
        self.quarter = lax.axis_index("dp")
        self.shard = lax.axis_index("fsdp")
        x = self.quarter % 2
        y = self.quarter // 2
        self.core = self.shard % 2
        self.z = self.shard // 2
        self.high = self.z // 2
        self.by_x = 2 * y + 1 - x
        self.by_y = 2 * (1 - y) + x
        self.across = 2 * (1 - y) + 1 - x
        self.sibling = (self.quarter, 2 * self.z + 1 - self.core)
        self.next_x = (self.by_x, self.shard)
        self.next_y = (self.by_y, self.shard)
        self.inner = (self.z > 0) & (self.z < 3)

    def at_z(self, z):
        return (self.quarter, 2 * z + self.core)


def transfer(source, target, send_sem, recv_sem, device):
    return pltpu.make_async_remote_copy(
        src_ref=source,
        dst_ref=target,
        send_sem=send_sem,
        recv_sem=recv_sem,
        device_id=device,
        device_id_type=pl.DeviceIdType.MESH,
    )


def greet(place, extra=()):
    barrier = pltpu.get_barrier_semaphore()

    def signal(device):
        pl.semaphore_signal(barrier, inc=1, device_id=device, device_id_type=pl.DeviceIdType.MESH)

    near = (place.sibling, place.next_x, place.next_y) + tuple(extra)
    for device in near:
        signal(device)

    @pl.when(place.z > 0)
    def _():
        signal(place.at_z(place.z - 1))

    @pl.when(place.z < 3)
    def _():
        signal(place.at_z(place.z + 1))

    pl.semaphore_wait(barrier, len(near) + 1 + (place.z + 1) // 2 % 2)


CUTS = 2
GATHER_SEMAPHORES = [
    pltpu.SemaphoreType.DMA((2 * CUTS,)),
    pltpu.SemaphoreType.DMA((3 * CUTS,)),
    pltpu.SemaphoreType.DMA((4 * CUTS,)),
    pltpu.SemaphoreType.DMA((12 * CUTS,)),
    pltpu.SemaphoreType.DMA((12 * CUTS,)),
    pltpu.SemaphoreType.DMA((1 + 18 * CUTS,)),
    pltpu.SemaphoreType.DMA((1 + 18 * CUTS,)),
    pltpu.SemaphoreType.DMA((8,)),
    pltpu.SemaphoreType.DMA((2 * CUTS,)),
    pltpu.SemaphoreType.DMA((3 * CUTS,)),
    pltpu.SemaphoreType.DMA((4 * CUTS,)),
]


class Gather:
    def __init__(self, full, out, sems):
        self.place = place = Place()
        self.full, self.out = full, out
        (
            self.own_send,
            self.relay_send,
            self.z_recv,
            self.xy_send,
            self.xy_recv,
            self.core_send,
            self.core_recv,
            self.out_sems,
            self.own_more,
            self.relay_more,
            self.z_more,
        ) = sems
        self.quarter = full.shape[1] // 4
        self.cut = self.quarter // CUTS
        self.z_part = self.cut // 64 * 16
        self.first_part = ((self.cut - self.z_part) // 16 + 1) // 2 * 16
        self.last_part = self.cut - self.z_part - self.first_part
        z = place.z
        self.origins = (z + 1 - 2 * (z % 2), 2 - place.high, 3 * (1 - place.high))
        self.relays = (3 - z, 3 * (z - 1), 3 * (z - 1))

    def region(self, which, start, size):
        return self.full.at[which, pl.ds(pl.multiple_of(start, 16), size)]

    def pieces(self, which, turn):
        place, quarter, cut, part = self.place, self.quarter, self.cut, self.first_part
        skip = turn % CUTS * cut
        return (
            self.region(which, place.quarter * quarter + skip, cut),
            self.region(which, place.by_x * quarter + skip, cut),
            self.region(which, place.by_y * quarter + skip, cut),
            self.region(which, place.across * quarter + skip, part),
            self.region(which, place.across * quarter + skip + part, self.last_part),
            self.region(which, place.across * quarter + skip + cut - self.z_part, self.z_part),
        )

    def own_copy(self, side, cut, more=False):
        place = self.place
        mine = self.pieces(place.shard, cut)[5 if more else 0]
        device = place.at_z(place.z - 1 + 2 * side)
        send, recv = (self.own_more, self.z_more) if more else (self.own_send, self.z_recv)
        return transfer(
            mine, mine, send.at[side * CUTS + cut], recv.at[place.z * CUTS + cut], device
        )

    def core_copy(self, index, ref):
        return transfer(ref, ref, self.core_send.at[index], self.core_recv.at[index], self.place.sibling)

    def xy_copy(self, index, ref, device):
        return transfer(ref, ref, self.xy_send.at[index], self.xy_recv.at[index], device)

    def store(self, index, which):
        return pltpu.make_async_copy(self.full.at[which], self.out.at[which], self.out_sems.at[index])

    def mirrored(self, step):
        return 2 * self.origins[step] + 1 - self.place.core

    def held(self, step):
        return 2 * self.origins[step] + self.place.core

    def start(self):
        place = self.place
        greet(place)
        for cut in range(CUTS):

            for more in (False, True):

                @pl.when(place.z > 0)
                def _():
                    self.own_copy(0, cut, more).start()

                @pl.when(place.z < 3)
                def _():
                    self.own_copy(1, cut, more).start()

        self.core_copy(0, self.full.at[place.shard]).start()
        self.store(0, place.shard).start()

    def relay(self, turn, more=False):
        step = turn // CUTS
        piece = self.pieces(self.held(step), turn)[5 if more else 0]
        device = self.place.at_z(self.relays[step])
        send, recv = (self.relay_more, self.z_more) if more else (self.relay_send, self.z_recv)
        sem = recv.at[self.origins[step] * CUTS + turn % CUTS]
        return transfer(piece, piece, send.at[turn], sem, device)

    def along_z(self, turn):
        place = self.place
        self.relay(turn).wait_recv()

        @pl.when(place.inner)
        def _():
            self.relay(turn).start()

        pieces = self.pieces(self.held(turn // CUTS), turn)
        self.xy_copy(4 * turn, pieces[0], place.next_x).start()
        self.xy_copy(4 * turn + 1, pieces[0], place.next_y).start()
        self.core_copy(1 + 6 * turn, pieces[0]).start()
        self.relay(turn, True).wait_recv()

        @pl.when(place.inner)
        def _():
            self.relay(turn, True).start()

        self.core_copy(6 + 6 * turn, pieces[5]).start()

    def along_xy(self, turn):
        place, part = self.place, self.first_part
        _, by_x, by_y, *_ = self.pieces(self.held(turn // CUTS), turn)
        self.xy_copy(4 * turn, by_x, place.next_x).wait_recv()
        self.xy_copy(4 * turn + 2, by_x.at[pl.ds(0, part)], place.next_y).start()
        self.core_copy(2 + 6 * turn, by_x).start()
        self.xy_copy(4 * turn + 1, by_y, place.next_y).wait_recv()
        self.xy_copy(4 * turn + 3, by_y.at[pl.ds(part, self.last_part)], place.next_x).start()
        self.core_copy(3 + 6 * turn, by_y).start()

    def across(self, turn):
        place = self.place
        step = turn // CUTS
        _, _, _, first, last, _ = self.pieces(self.held(step), turn)
        self.xy_copy(4 * turn + 2, first, place.next_y).wait_recv()
        self.core_copy(4 + 6 * turn, first).start()
        self.xy_copy(4 * turn + 3, last, place.next_x).wait_recv()
        self.core_copy(5 + 6 * turn, last).start()
        if turn % CUTS == CUTS - 1:
            self.store(2 + 2 * step, self.held(step)).start()

    def core_own(self):
        which = 2 * self.place.z + 1 - self.place.core
        self.core_copy(0, self.full.at[which]).wait_recv()
        self.store(1, which).start()

    def core(self, step):
        which = self.mirrored(step)
        for turn in range(step * CUTS, (step + 1) * CUTS):
            for index, ref in enumerate(self.pieces(which, turn)):
                self.core_copy(1 + 6 * turn + index, ref).wait_recv()
        self.store(3 + 2 * step, which).start()

    def finish(self):
        place = self.place
        for cut in range(CUTS):

            for more in (False, True):

                @pl.when(place.z > 0)
                def _():
                    self.own_copy(0, cut, more).wait_send()

                @pl.when(place.z < 3)
                def _():
                    self.own_copy(1, cut, more).wait_send()

        self.core_copy(0, self.full.at[place.shard]).wait_send()
        self.store(0, place.shard).wait()
        self.store(1, 2 * place.z + 1 - place.core).wait()
        for turn in range(3 * CUTS):

            @pl.when(place.inner)
            def _():
                self.relay(turn).wait_send()
                self.relay(turn, True).wait_send()

            pieces = self.pieces(self.held(turn // CUTS), turn)
            self.xy_copy(4 * turn, pieces[0], place.next_x).wait_send()
            self.xy_copy(4 * turn + 1, pieces[0], place.next_y).wait_send()
            self.xy_copy(4 * turn + 2, pieces[3], place.next_y).wait_send()
            self.xy_copy(4 * turn + 3, pieces[4], place.next_x).wait_send()
            for index, ref in enumerate(pieces):
                self.core_copy(1 + 6 * turn + index, ref).wait_send()
        for step in range(3):
            self.store(2 + 2 * step, self.held(step)).wait()
            self.store(3 + 2 * step, self.mirrored(step)).wait()


def gather_kernel(master_ref, out_ref, full, *sems):
    gather = Gather(full, out_ref, sems)
    full[gather.place.shard] = master_ref[...].astype(BF16)
    gather.start()
    turns = 3 * CUTS
    for turn in range(turns + 2):
        if turn < turns:
            gather.along_z(turn)
        if 1 <= turn <= turns:
            gather.along_xy(turn - 1)
        if turn >= 2:
            gather.across(turn - 2)
        if turn == 2:
            gather.core_own()
        if turn >= 4 and turn % CUTS == 0:
            gather.core(turn // CUTS - 2)
    gather.core(2)
    gather.finish()


def gather_shards(master):
    rows = master.shape[0] * BLK
    shards = lax.axis_size("fsdp")
    return pl.pallas_call(
        gather_kernel,
        in_specs=[pl.BlockSpec(memory_space=pltpu.VMEM)],
        out_specs=pl.BlockSpec(memory_space=pltpu.HBM),
        out_shape=jax.ShapeDtypeStruct((shards, rows, BLK), BF16),
        scratch_shapes=[pltpu.VMEM((shards, rows, BLK), BF16)] + GATHER_SEMAPHORES,
        compiler_params=pltpu.CompilerParams(
            collective_id=0, has_side_effects=True, vmem_limit_bytes=60 * MIB
        ),
        cost_estimate=pl.CostEstimate(flops=0, bytes_accessed=200 * MIB, transcendentals=0),
        name="gather",
    )(master.reshape(rows, BLK)).reshape(-1, BLK, BLK)


def add_rows(target, former, latter, rows, step):
    @pl.loop(0, rows // step)
    def _(index):
        part = pl.ds(pl.multiple_of(index * step, 16), step)
        target[part] = (former[part].astype(F32) + latter[part].astype(F32)).astype(BF16)


def reduce_scratch(rows):
    quarter = rows // 4
    half = quarter // 2
    return [
        pltpu.VMEM((4, rows, BLK), BF16),
        pltpu.VMEM((4, rows, BLK), BF16),
        pltpu.VMEM((4, 2, half, BLK), BF16),
        pltpu.VMEM((4, 2, half, BLK), BF16),
        pltpu.VMEM((4, half, BLK), BF16),
        pltpu.VMEM((4, half, BLK), BF16),
        pltpu.VMEM((5, quarter, BLK), BF16),
        pltpu.VMEM((rows, BLK), BF16),
        pltpu.SemaphoreType.DMA((4,)),
        pltpu.SemaphoreType.DMA((4,)),
        pltpu.SemaphoreType.DMA((4,)),
        pltpu.SemaphoreType.DMA((24,)),
        pltpu.SemaphoreType.DMA((24,)),
        pltpu.SemaphoreType.DMA((3,)),
        pltpu.SemaphoreType.DMA((5,)),
        pltpu.SemaphoreType.DMA((4,)),
        pltpu.SemaphoreType.DMA((4,)),
    ]


class Reduce:
    def __init__(self, terms, base, out, scratch):
        self.place = place = Place()
        self.terms, self.base, self.out = terms, base, out
        (
            self.mine,
            self.sib,
            self.from_x,
            self.from_y,
            self.late_y,
            self.late_x,
            self.from_z,
            self.result,
            self.load_sems,
            self.core_send,
            self.core_recv,
            self.xy_send,
            self.xy_recv,
            self.z_send,
            self.z_recv,
            self.last_send,
            self.last_recv,
        ) = scratch
        self.quarter = out.shape[0] // 4
        self.half = self.quarter // 2
        z, high = place.z, place.high
        low = 1 - high
        self.order = (3 * low, low * (2 - 2 * z) + high * (7 - 2 * z), 1 + z % 2, z)
        self.onward = (z + 1 - 2 * high, z + 1 - 2 * (z % 2), z + 1 - 2 * high)
        self.closing = (0, (z % 2) * low, high)
        self.far = place.at_z(z + 2 - 4 * high)
        self.near = place.at_z(z + 1 - 2 * (z % 2))

    def shard_terms(self, shard):
        rows = self.out.shape[0]
        return self.terms.at[pl.ds(pl.multiple_of(self.base + shard * rows, 16), rows)]

    def load(self, step):
        source = self.shard_terms(2 * self.order[step] + self.place.core)
        return pltpu.make_async_copy(source, self.mine.at[step], self.load_sems.at[step])

    def core_copy(self, step):
        return transfer(
            self.shard_terms(2 * self.order[step] + 1 - self.place.core),
            self.sib.at[step],
            self.core_send.at[step],
            self.core_recv.at[step],
            self.place.sibling,
        )

    def part(self, step, which, side):
        start = pl.multiple_of(which * self.quarter + side * self.half, 16)
        return self.mine.at[step, pl.ds(start, self.half)]

    def xy_copy(self, step, index):
        place = self.place
        source, target, device = (
            (self.part(step, place.by_x, 0), self.from_x.at[step, 0], place.next_x),
            (self.part(step, place.across, 0), self.from_x.at[step, 1], place.next_x),
            (self.part(step, place.by_y, 1), self.from_y.at[step, 0], place.next_y),
            (self.part(step, place.across, 1), self.from_y.at[step, 1], place.next_y),
            (self.part(step, place.by_y, 0), self.late_y.at[step], place.next_y),
            (self.part(step, place.by_x, 1), self.late_x.at[step], place.next_x),
        )[index]
        place = 6 * step + index
        return transfer(source, target, self.xy_send.at[place], self.xy_recv.at[place], device)

    def start(self):
        greet(self.place, (self.far,))
        for step in range(2):
            self.core_copy(step).start()
        for step in range(4):
            self.load(step).start()

    def core(self, step):
        place, quarter = self.place, self.quarter
        self.load(step).wait()
        self.core_copy(step).wait_recv()
        if step < 2:
            self.core_copy(step + 2).start()

        def add(which):
            block = pl.ds(pl.multiple_of(which * quarter, 16), quarter)
            mine = self.mine.at[step, block]
            add_rows(mine, mine, self.sib.at[step, block], quarter, self.half)

        add(place.by_x)
        add(place.across)
        self.xy_copy(step, 0).start()
        self.xy_copy(step, 1).start()
        add(place.by_y)
        self.xy_copy(step, 2).start()
        self.xy_copy(step, 3).start()
        add(place.quarter)

    def take(self, step, which, side, index, source):
        self.xy_copy(step, index).wait_recv()
        target = self.part(step, which, side)
        add_rows(target, target, source, self.half, self.half)

    def first(self, step):
        place = self.place
        self.take(step, place.by_y, 0, 1, self.from_x.at[step, 1])
        self.xy_copy(step, 4).start()
        self.take(step, place.by_x, 1, 3, self.from_y.at[step, 1])
        self.xy_copy(step, 5).start()
        self.take(step, place.quarter, 0, 0, self.from_x.at[step, 0])
        self.take(step, place.quarter, 1, 2, self.from_y.at[step, 0])

    def own_block(self, step):
        return self.mine.at[step, pl.ds(pl.multiple_of(self.place.quarter * self.quarter, 16), self.quarter)]

    def z_copy(self, step):
        goal = self.order[step]
        slot = goal + self.closing[step] * (4 - goal)
        return transfer(
            self.own_block(step),
            self.from_z.at[slot],
            self.z_send.at[step],
            self.z_recv.at[slot],
            self.place.at_z(self.onward[step]),
        )

    def take_z(self, step, slot):
        source = self.from_z.at[slot]
        transfer(source, source, self.z_send.at[0], self.z_recv.at[slot], self.near).wait_recv()
        block = self.own_block(step)
        add_rows(block, block, source, self.quarter, self.half)

    def second(self, step):
        place = self.place
        self.take(step, place.quarter, 0, 4, self.late_y.at[step])
        self.take(step, place.quarter, 1, 5, self.late_x.at[step])
        if step < 3:

            @pl.when(place.inner)
            def _():
                self.take_z(step, self.order[step])

            self.z_copy(step).start()
        else:

            @pl.when(place.z > 0)
            def _():
                self.take_z(step, place.z)

            @pl.when(place.z < 3)
            def _():
                self.take_z(step, 4)

    def final(self, which, side=None):
        start = pl.multiple_of(which * self.quarter + (0 if side is None else side * self.half), 16)
        return self.result.at[pl.ds(start, self.quarter if side is None else self.half)]

    def last_copy(self, index, ref):
        device = (self.place.next_x, self.place.next_y, self.place.next_y, self.place.next_x)[index]
        return transfer(ref, ref, self.last_send.at[index], self.last_recv.at[index], device)

    def share(self):
        own = self.final(self.place.quarter)
        own[...] = self.own_block(3)[...]
        self.last_copy(0, own).start()
        self.last_copy(1, own).start()

    def share_on(self):
        place = self.place
        self.last_copy(0, self.final(place.by_x)).wait_recv()
        self.last_copy(2, self.final(place.by_x, 0)).start()
        self.last_copy(1, self.final(place.by_y)).wait_recv()
        self.last_copy(3, self.final(place.by_y, 1)).start()

    def finish(self):
        place = self.place
        self.last_copy(2, self.final(place.across, 0)).wait_recv()
        self.last_copy(3, self.final(place.across, 1)).wait_recv()
        self.out[...] = self.result[...]
        for step in range(4):
            self.core_copy(step).wait_send()
            for index in range(6):
                self.xy_copy(step, index).wait_send()
            if step < 3:
                self.z_copy(step).wait_send()
        own = self.final(place.quarter)
        self.last_copy(0, own).wait_send()
        self.last_copy(1, own).wait_send()
        self.last_copy(2, self.final(place.by_x, 0)).wait_send()
        self.last_copy(3, self.final(place.by_y, 1)).wait_send()


def reduce_kernel(*refs, base, short_steps):
    terms, small_ref, d_ref, resid_ref, w_ref, out_ref, small_out, short_ref, long_ref = refs[:9]
    small_in, small_sum, small_send, small_recv = refs[9:13]
    reduce = Reduce(terms, base, out_ref, refs[13:])
    place = reduce.place
    partners = (place.sibling, place.next_x, place.next_y, reduce.near, reduce.far)

    def small_copy(level):
        return transfer(
            small_sum.at[level],
            small_in.at[level],
            small_send.at[level],
            small_recv.at[level],
            partners[level],
        )

    def small_start():
        small_sum[0] = small_ref[...]
        small_copy(0).start()

    def small_step(level):
        small_copy(level - 1).wait_recv()
        small_sum[level] = small_sum[level - 1] + small_in[level - 1]
        if level < 5:
            small_copy(level).start()
        else:
            small_out[...] = small_sum[5]

    run_events(
        pl.program_id(0),
        (
            (reduce.start, small_start),
            (partial(reduce.core, 0), partial(small_step, 1)),
            (partial(reduce.core, 1), partial(reduce.first, 0), partial(small_step, 2)),
            (
                partial(reduce.core, 2),
                partial(reduce.first, 1),
                partial(reduce.second, 0),
                partial(small_step, 3),
            ),
            (
                partial(reduce.core, 3),
                partial(reduce.first, 2),
                partial(reduce.second, 1),
                partial(small_step, 4),
            ),
            (partial(reduce.first, 3), partial(reduce.second, 2), partial(small_step, 5)),
            (partial(reduce.second, 3), reduce.share),
            (reduce.share_on,),
        ),
    )
    input_product(d_ref, resid_ref, w_ref, short_ref, long_ref, short_steps)

    @pl.when(pl.program_id(0) == pl.num_programs(0) - 1)
    def _():
        reduce.finish()
        for level in range(5):
            small_copy(level).wait_send()


def reduce_late(terms, base, rows, small, d_qkv, resid, w_qkv, short_tiles):
    steps = resid.shape[0] // INPUT_ROWS
    short_steps = short_tiles * TILE // INPUT_ROWS
    in_specs, out_specs = input_specs(short_steps)

    def whole(shape):
        return pl.BlockSpec(shape, lambda step: (0, 0), pipeline_mode=pl.Buffered(1))

    return pl.pallas_call(
        partial(reduce_kernel, base=base, short_steps=short_steps),
        grid=(steps,),
        in_specs=[pl.BlockSpec(memory_space=pltpu.HBM), whole(small.shape)] + in_specs,
        out_specs=[
            pl.BlockSpec((rows, BLK), lambda step: (0, 0)),
            pl.BlockSpec(small.shape, lambda step: (0, 0)),
        ]
        + out_specs,
        out_shape=[
            jax.ShapeDtypeStruct((rows, BLK), BF16),
            jax.ShapeDtypeStruct((SMALL_ROWS, BLK), F32),
            jax.ShapeDtypeStruct((short_steps * INPUT_ROWS, D), F32),
            jax.ShapeDtypeStruct(((steps - short_steps) * INPUT_ROWS, D), F32),
        ],
        scratch_shapes=[
            pltpu.VMEM((5, SMALL_ROWS, BLK), F32),
            pltpu.VMEM((6, SMALL_ROWS, BLK), F32),
            pltpu.SemaphoreType.DMA((5,)),
            pltpu.SemaphoreType.DMA((5,)),
        ]
        + reduce_scratch(rows),
        compiler_params=pltpu.CompilerParams(
            collective_id=3, has_side_effects=True, vmem_limit_bytes=60 * MIB
        ),
        cost_estimate=pl.CostEstimate(flops=0, bytes_accessed=200 * MIB, transcendentals=0),
        name="reduce",
    )(terms, small, d_qkv, resid, w_qkv)


def count_where(condition, axis):
    return jnp.sum(condition.astype(jnp.int32), axis=axis)


def slot_codes(slots, qkv_slots, slot_count, shards):
    early = slot_count - LATE
    shard = slots // slot_count
    begin = shard * slot_count
    inside = (qkv_slots[None, :] >= begin[:, None]) & (qkv_slots[None, :] < (begin + slot_count)[:, None])
    own = count_where(qkv_slots[None, :] == slots[:, None], 1)
    before = count_where(inside & (qkv_slots[None, :] < slots[:, None]), 1)
    number = count_where(inside, 1)
    position = jnp.where(own > 0, slot_count - number + before, slots - begin - before)
    code = jnp.where(
        position < early,
        shard * early + position,
        shards * early + shard * LATE + position - early,
    )
    return code, position, jnp.max(number)


def update_kernel(
    position_ref,
    held_ref,
    early,
    late,
    master,
    left_stat,
    right_stat,
    left_root,
    right_root,
    slot_grad,
    new_left,
    new_right,
    new_master,
):
    count = master.shape[0]
    first = pl.program_id(0) * count
    split = early.shape[0] // BLK

    def block(ref, place):
        return ref[pl.ds(pl.multiple_of(place * BLK, BLK), BLK)]

    def grad_of(index):
        place = position_ref[first + index]
        grad = jnp.where(
            place < split,
            block(early, jnp.minimum(place, split - 1)),
            block(late, jnp.maximum(place - split, 0)),
        )
        return jnp.where(held_ref[first + index] > 0, grad, jnp.zeros_like(grad))

    for begin in range(0, count, 4):
        some = range(begin, min(begin + 4, count))
        grads = [grad_of(index) for index in some]
        applied = [product(left_root[index].astype(BF16), grad) for index, grad in zip(some, grads)]
        outer_left = [right_product(grad, grad) for grad in grads]
        outer_right = [left_product(grad, grad) for grad in grads]
        totals = [
            product(part.astype(BF16), right_root[index].astype(BF16)) for index, part in zip(some, applied)
        ]
        for place, index in enumerate(some):
            slot_grad[index] = grads[place].astype(F32)
            new_left[index] = STAT_DECAY * left_stat[index] + (1.0 - STAT_DECAY) * outer_left[place]
            new_right[index] = STAT_DECAY * right_stat[index] + (1.0 - STAT_DECAY) * outer_right[place]
            new_master[index] = master[index] - MATRIX_RATE * totals[place]


def update(position, held, early, late, master, left_stat, right_stat, left_root, right_root):
    slot_count = master.shape[0]
    group = max(size for size in range(1, 12) if slot_count % size == 0)
    some = pl.BlockSpec((group, BLK, BLK), lambda step, *_: (step, 0, 0))

    def whole(shape):
        return pl.BlockSpec(shape, lambda step, *_: (0, 0), pipeline_mode=pl.Buffered(1))

    return pl.pallas_call(
        update_kernel,
        grid_spec=pltpu.PrefetchScalarGridSpec(
            num_scalar_prefetch=2,
            grid=(slot_count // group,),
            in_specs=[whole(early.shape), whole(late.shape)] + [some] * 5,
            out_specs=[some] * 4,
        ),
        out_shape=[jax.ShapeDtypeStruct(master.shape, F32)] * 4,
        compiler_params=pltpu.CompilerParams(vmem_limit_bytes=60 * MIB),
        cost_estimate=pl.CostEstimate(
            flops=8 * slot_count * BLK**3, bytes_accessed=36 * slot_count * BLK**2, transcendentals=0
        ),
        name="update",
    )(position, held, early, late, master, left_stat, right_stat, left_root, right_root)


def body(
    x_short,
    x_long,
    cot_short,
    cot_long,
    logit_cot_short,
    logit_cot_long,
    len_short,
    len_long,
    block_slot,
    master,
    left_stat,
    right_stat,
    left_root,
    right_root,
    small_params,
    small_first,
    small_second,
    own_transfers,
):
    slot_count = master.shape[0]
    shards = lax.axis_size("fsdp")
    all_slots = slot_count * shards
    short_seqs, width = x_short.shape[:2]
    long_seqs = x_long.shape[0]
    short_tiles = short_seqs * width // TILE
    per_tile = TILE // width

    own = jnp.arange(slot_count, dtype=jnp.int32) + slot_count * lax.axis_index("fsdp")
    held = jnp.any(block_slot[None, :] == own[:, None], axis=1).astype(jnp.int32)
    if own_transfers:
        early_count = slot_count - LATE
        code, position, most = slot_codes(
            jnp.concatenate([block_slot, own]), block_slot[: 3 * 36], slot_count, shards
        )
        position = position[NBLK:]
        code = code[:NBLK]
        fits = most <= LATE
        gathered = gather_shards(master)
    else:
        gathered = lax.all_gather(master.astype(BF16), "fsdp", axis=0, tiled=True)
    w_qkv = assemble(block_slot, gathered)
    pieces = unpack(small_params)
    params = jnp.pad(small_params, (0, SMALL_ROWS * BLK - small_params.shape[0])).reshape(SMALL_ROWS, BLK)
    w_class = pieces[-2].reshape(SD, NCLS)
    b_class = pieces[-1].reshape(1, NCLS)
    x, *qkv, context, probs_short, probs_long = attention(
        len_short,
        len_long,
        x_short.reshape(-1, D),
        x_long.reshape(-1, D),
        params,
        w_qkv,
        short_tiles,
        width,
    )

    (
        enc_short,
        enc_long,
        logits_short,
        logits_long,
        first,
        active,
        d_up,
        d_down,
        d_branch,
        d_context,
        d_resid,
        g_student,
        g_hidden,
        g_small,
    ) = feed(
        len_short,
        len_long,
        block_slot,
        x,
        context,
        cot_short.reshape(-1, D),
        cot_long.reshape(-1, D),
        (logit_cot_short, logit_cot_long),
        (params, w_class, b_class),
        gathered,
        short_tiles,
        width,
    )
    g_out = left_product(context, d_branch).astype(BF16)
    others = (g_out, g_student.astype(BF16), g_hidden.astype(BF16))
    if own_transfers:
        terms = feed_grads(code, first, d_down, active, d_up, others, all_slots)
        *back, early_reduced = attention_back(
            qkv,
            probs_short,
            probs_long,
            d_context,
            x,
            short_tiles,
            terms.reshape(-1, BLK),
            early_count * BLK,
        )
    else:
        back = attention_back(qkv, probs_short, probs_long, d_context, x, short_tiles)
    d_qkv, g_b_query, g_b_value, x_turned = back

    def reduce_all():
        slot_terms = feed_grads(block_slot, first, d_down, active, d_up, others, all_slots)
        slot_terms, small_terms = input_weights(
            block_slot, x_turned, d_qkv, g_small, g_b_query, g_b_value, slot_terms
        )
        reduced = lax.psum_scatter(slot_terms, "fsdp", scatter_dimension=0, tiled=True)
        return lax.psum(reduced, "dp").reshape(-1, BLK), small_terms

    def renew(places, early, late):
        return update(
            places, held, early, late, master, left_stat, right_stat, left_root, right_root
        )

    def renew_all(blocks):
        return renew(jnp.arange(slot_count, dtype=jnp.int32), blocks, blocks)

    if own_transfers:
        terms, small_terms = input_weights(code, x_turned, d_qkv, g_small, g_b_query, g_b_value, terms)
        late_reduced, small_total, in_short, in_long = reduce_late(
            terms.reshape(-1, BLK),
            shards * early_count * BLK,
            LATE * BLK,
            small_terms,
            d_qkv,
            d_resid,
            w_qkv,
            short_tiles,
        )

        updated = lax.cond(
            fits,
            lambda: renew(position, early_reduced, late_reduced),
            lambda: renew_all(reduce_all()[0]),
        )
    else:
        in_short, in_long = input_grads(d_qkv, d_resid, w_qkv, short_tiles)
        blocks, small_terms = reduce_all()
        updated = renew_all(blocks)
        small_total = lax.psum(small_terms, ("dp", "fsdp"))
    slot_grad, new_left, new_right, new_master = updated
    small_grad = jnp.concatenate(
        [
            small_total[:CLASS_ROW].reshape(-1),
            small_total[CLASS_ROW : CLASS_ROW + NCLS].T.reshape(-1),
            small_total[LAST_ROW, :NCLS],
        ]
    )
    new_first = BETA_ONE * small_first + (1.0 - BETA_ONE) * small_grad
    new_second = BETA_TWO * small_second + (1.0 - BETA_TWO) * small_grad * small_grad
    first_hat = new_first / (1.0 - BETA_ONE**STEP)
    second_hat = new_second / (1.0 - BETA_TWO**STEP)
    new_small = small_params - ADAM_RATE * first_hat / (jnp.sqrt(second_hat) + ADAM_EPSILON)
    return (
        enc_short.reshape(x_short.shape),
        logits_short,
        enc_long.reshape(x_long.shape),
        logits_long,
        in_short.reshape(x_short.shape),
        in_long.reshape(x_long.shape),
        slot_grad,
        new_left,
        new_right,
        new_master,
        new_first,
        new_second,
        new_small,
    )


def solution(mesh):
    both = ("dp", "fsdp")
    placed = (
        P(both, None, None),
        P(both, None, None),
        P(both, None, None),
        P(both, None, None),
        P(both, None),
        P(both, None),
        P(both),
        P(both),
        P(),
        P("fsdp", None, None),
        P("fsdp", None, None),
        P("fsdp", None, None),
        P("fsdp", None, None),
        P("fsdp", None, None),
        P(),
        P(),
        P(),
    )
    return jax.shard_map(
        partial(body, own_transfers=(mesh.shape["dp"], mesh.shape["fsdp"]) == (4, 8)),
        mesh=mesh,
        in_specs=placed,
        out_specs=(
            P(both, None, None),
            P(both, None),
            P(both, None, None),
            P(both, None),
            P(both, None, None),
            P(both, None, None),
            P("fsdp", None, None),
            P("fsdp", None, None),
            P("fsdp", None, None),
            P("fsdp", None, None),
            P(),
            P(),
            P(),
        ),
        check_vma=False,
    )
```

profile of v0, /device:TPU:8, one launch (start us, length us, event | category | flops | bytes accessed | tf_op | source)
XLA Modules:
  0.0 399.1 jit_solution(4046269404309139113)
XLA Ops:
  7.2 0.9 compare_reduce_fusion
  8.1 1.2 slice_bitcast_fusion.3.b_class_ref
  9.3 0.7 slice.27
  10.0 0.8 broadcast_multiply_fusion
  10.7 0.2 convert_reduce_fusion.1
  10.9 1.2 add_select_fusion.1
  12.8 0.7 slice.25
  13.5 1.4 pad_bitcast_fusion.params
  15.0 0.8 reshape.157.w_class_ref
  15.7 0.0 copy-start.6
  15.7 57.5 %gather.1 = bf16[8,7040,128]{2,1,0:T(8,128)(2,1)} custom-call(f32[7040,128]{1,0:T(8,128)} %bitcast.30), custom_call_target="tpu_custom_call" | custom-call | bytes 209715200 | tf_op jit(solution)/shard_map/gather/pallas_call | solution.py:1325
  73.2 0.0 copy-done.6
  73.2 4.3 %assemble.1.w_ref.refs_4_ = bf16[768,2304]{1,0:T(8,128)(2,1)} custom-call(s32[439]{0:T(512)S(1)} %copy-done.6, bf16[440,128,128]{2,1,0:T(8,128)(2,1)} %bitcast.28), custom_call_target="tpu_custom_call" | custom-call | tf_op jit(solution)/shard_map/assemble/pallas_call | solution.py:96
  77.5 32.1 %attention.1 = (bf16[2048,768]{1,0:T(8,128)(2,1)}, bf16[2048,768]{1,0:T(8,128)(2,1)}, bf16[2048,768]{1,0:T(8,128)(2,1)}, bf16[2048,768]{1,0:T(8,128)(2,1)}, bf16...) custom-call(s32[8]{0:T(128)} %len_short.3, s32[2]{0:T(128)} %len_long.3, ...), custom_call_target="tpu_custom_call" | custom-call | flops 10468982784 | bytes 36700160 | tf_op jit(solution)/shard_map/attention/pallas_call | solution.py:485
  109.7 96.3 %feed.1 = (bf16[1024,768]{1,0:T(8,128)(2,1)}, bf16[1024,768]{1,0:T(8,128)(2,1)}, f32[8,14]{1,0:T(8,128)}, f32[2,14]{1,0:T(2,128)}, bf16[768,2048]{1,0:T(8,128)(2...) custom-call(s32[8]{0:T(128)} %len_short.3, ...), custom_call_target="tpu_custom_call" | custom-call | flops 43486543872 | bytes 73400320 | tf_op jit(solution)/shard_map/feed/pallas_call | solution.py:990
  206.0 0.0 copy-start.3
  206.0 0.0 copy-start.1
  206.0 5.6 %convolution_convert_fusion.g_out = bf16[768,768]{1,0:T(8,128)(2,1)S(1)} fusion(bf16[2048,768]{1,0:T(8,128)(2,1)} %get-tuple-element.136.context_ref, bf16[2048,768]{1,0:T(8,128)(2,1)} %get-tuple-element.151), kind=kOutput, calls=%fused_computation | convolution fusion | flops 2416508928 | bytes 7471104 | tf_op jit(solution)/shard_map/dot_general | solution.py:43
  211.5 0.0 copy-start.8
  211.6 0.0 copy-done.3
  211.6 0.0 copy-done.1
  211.6 0.0 copy-start.7
  211.6 27.7 %feed_grads.3._ = bf16[440,128,128]{2,1,0:T(8,128)(2,1)} custom-call(s32[439]{0:T(512)} %bitcast.34, bf16[768,2048]{1,0:T(8,128)(2,1)} %get-tuple-element.147.first_turned, bf16[768,2048]{1,0:T(8,128)(2,1)} %get-tuple-element.148.down_turned, bf16[2048,3072]{1,0:T(8,128)(2,1)} %get-tuple-element.149.active_ref, ...), custom_call_target="tpu_custom_call" | custom-call | flops 19327352832 | bytes 52428800 | tf_op jit(solution)/shard_map/feed_grads/pallas_call | solution.py:190
  239.3 0.0 copy-done.8
  239.3 0.0 copy-done.7
  239.3 62.5 %attention_back.1 = (bf16[2048,2304]{1,0:T(8,128)(2,1)}, f32[1,768]{1,0:T(1,128)S(1)}, f32[1,768]{1,0:T(1,128)S(1)}, bf16[768,2048]{1,0:T(8,128)(2,1)S(1)}, bf16[3968,128]{1,0:T(8,128)(2,1)}) custom-call(bf16[2048,768]{1,0:T(8,128)(2,1)} %get-tuple-element.141.refs_0_, bf16[2048,768]{1,0:T(8,128)(2,1)} %get-tuple-element.142.refs_1_, ...), custom_call_target="tpu_custom_call" | custom-call | flops 8053063680 | bytes 52428800 | tf_op jit(solution)/shard_map/attention_back/pallas_call | solution.py:640
  301.9 12.2 %input_weights.3 = (bf16[440,128,128]{2,1,0:T(8,128)(2,1)}, f32[96,128]{1,0:T(8,128)}) custom-call(s32[439]{0:T(512)} %bitcast.35, bf16[768,2048]{1,0:T(8,128)(2,1)S(1)} %get-tuple-element.154.turned, bf16[2048,2304]{1,0:T(8,128)(2,1)} %get-tuple-element.155.d_ref.refs_2_, ...), custom_call_target="tpu_custom_call", output_to_operand_aliasing={{0}: (6, {})} | custom-call | flops 7247757312 | bytes 16777216 | tf_op jit(solution)/shard_map/input_weights/pallas_call | solution.py:251
  314.1 54.5 %reduce.1 = (bf16[3072,128]{1,0:T(8,128)(2,1)}, f32[96,128]{1,0:T(8,128)}, f32[1024,768]{1,0:T(8,128)}, f32[1024,768]{1,0:T(8,128)}) custom-call(bf16[56320,128]{1,0:T(8,128)(2,1)} %bitcast.27, f32[96,128]{1,0:T(8,128)} %get-tuple-element.160.refs_1_, bf16[2048,2304]{1,0:T(8,128)(2,1)} %get-tuple-element.155.d_ref.refs_2_, ...), custom_call_target="tpu_custom_call" | custom-call | bytes 209715200 | tf_op jit(solution)/shard_map/reduce/pallas_call | solution.py:1627
  368.6 0.0 copy-start.4
  368.6 0.0 copy-start.2
  368.6 0.0 copy-start.5
  368.7 16.0 %conditional.1 = ((f32[55,128,128]{2,1,0:T(8,128)}, f32[55,128,128]{2,1,0:T(8,128)}, f32[55,128,128]{2,1,0:T(8,128)}, f32[55,128,128]{2,1,0:T(8,128)})) conditional(s32[]{:T(128)} %convert_element_type.32, (s32[439]{0:T(512)S(1)}, bf16[768,2048]{1,0:T(8,128)(2,1)}, bf16[768,2048]{1,0:T(8,128)(2,1)}, bf16[2048,3072]{1,0:T(8,128)(2,1)}, ...), branch_computations={%region_5.8_spmd, %region_8.9_spmd} | conditional | flops 27498758144 | bytes 161120576 | solution.py:1883
  368.7 1.3 slice.17.position_ref
  370.0 14.7 %update.3 = (f32[55,128,128]{2,1,0:T(8,128)}, f32[55,128,128]{2,1,0:T(8,128)}, f32[55,128,128]{2,1,0:T(8,128)}, f32[55,128,128]{2,1,0:T(8,128)}) custom-call(s32[55]{0:T(128)} %slice.17.position_ref, s32[55]{0:T(128)S(1)} %get-tuple-element.78.held_ref, bf16[3968,128]{1,0:T(8,128)(2,1)} %get-tuple-element.79.early, ...), custom_call_target="tpu_custom_call" | custom-call | flops 922746880 | bytes 32440320 | tf_op jit(solution)/shard_map/cond/branch_1_fun/update/pallas_call | solution.py:1733
  384.7 0.0 copy-done.4
  384.7 0.1 copy.33
  384.8 0.1 reshape.166
  385.0 0.0 copy-done.2
  385.0 0.0 copy-done.5
  385.0 1.5 divide_subtract_fusion
  386.4 0.0 copy-start
  386.4 3.9 copy.47
  390.4 0.0 copy-done
  390.4 1.7 copy.48
  (8 shorter events, 0.1 us)
Async XLA Ops:
  15.7 57.5 %copy-start.6 = (s32[439]{0:T(512)S(1)}, s32[439]{0:T(512)}, u32[]{:S(2)}) copy-start(s32[439]{0:T(512)} %slot_ref.3) | copy-start | bytes 5272
  206.0 5.6 %copy-start.3 = (f32[128,128]{1,0:T(8,128)S(1)}, f32[128,128]{1,0:T(8,128)}, u32[]{:S(2)}) copy-start(f32[128,128]{1,0:T(8,128)} %get-tuple-element.153) | copy-start | bytes 196612
  206.0 5.6 %copy-start.1 = (f32[768,128]{1,0:T(8,128)S(1)}, f32[768,128]{1,0:T(8,128)}, u32[]{:S(2)}) copy-start(f32[768,128]{1,0:T(8,128)} %get-tuple-element.152) | copy-start | bytes 1179652
  211.5 27.8 %copy-start.8 = (bf16[768,768]{1,0:T(8,128)(2,1)}, bf16[768,768]{1,0:T(8,128)(2,1)S(1)}, u32[]{:S(2)}) copy-start(bf16[768,768]{1,0:T(8,128)(2,1)S(1)} %convolution_convert_fusion.g_out) | copy-start | bytes 3538948
  211.6 27.7 %copy-start.7 = (bf16[128,128]{1,0:T(8,128)(2,1)}, bf16[128,128]{1,0:T(8,128)(2,1)S(1)}, u32[]{:S(2)}) copy-start(bf16[128,128]{1,0:T(8,128)(2,1)S(1)} %convert_element_type.31.g_hidden) | copy-start | bytes 98308
  368.6 16.0 %copy-start.4 = (f32[96,128]{1,0:T(8,128)S(1)}, f32[96,128]{1,0:T(8,128)}, u32[]{:S(2)}) copy-start(f32[96,128]{1,0:T(8,128)} %get-tuple-element.170) | copy-start | bytes 147460
  368.6 16.3 %copy-start.2 = (f32[11406]{0:T(1024)S(1)}, f32[11406]{0:T(1024)}, u32[]{:S(2)}) copy-start(f32[11406]{0:T(1024)} %param.33) | copy-start | bytes 136876
  368.6 16.3 %copy-start.5 = (f32[11406]{0:T(1024)S(1)}, f32[11406]{0:T(1024)}, u32[]{:S(2)}) copy-start(f32[11406]{0:T(1024)} %param.35) | copy-start | bytes 136876
  386.4 3.9 copy-start
where the time goes:
time: 405 us; the launch traced here: 399 us
  Pallas kernels  362 us (89%)
  between operations  15.2 us (4%)
  local copies, waits for them, and re-layouts  11.9 us (3%)
  matrix products  5.56 us (1%)
  other arithmetic  4.58 us (1%)
    pallas_call x1, Pallas kernels, feed(): pl.pallas_call(partial(feed_kernel, short_tiles=short_tiles, width=width)...  96.3 us
    pallas_call x1, Pallas kernels, attention_back(): pl.pallas_call(partial(attention_back_kernel, short_tiles=short_tiles, tr...  62.5 us
    pallas_call x1, Pallas kernels, gather_shards(): pl.pallas_call(gather_kernel, in_specs=[pl.BlockSpec(memory_space=pltpu.V...  57.5 us
    pallas_call x1, Pallas kernels, reduce_late(): pl.pallas_call(partial(reduce_kernel, base=base, short_steps=short_steps)...  54.5 us
    pallas_call x1, Pallas kernels, attention(): pl.pallas_call(partial(attention_kernel, short_tiles=short_tiles), grid=(...  32.1 us
    pallas_call x1, Pallas kernels, feed_grads(): pl.pallas_call(feed_grads_kernel, grid_spec=pltpu.PrefetchScalarGridSpec(...  27.7 us
    pallas_call x1, Pallas kernels, update(): pl.pallas_call(update_kernel, grid_spec=pltpu.PrefetchScalarGridSpec(num_...  14.7 us
    pallas_call x1, Pallas kernels, input_weights(): pl.pallas_call(input_weights_kernel, grid_spec=pltpu.PrefetchScalarGridSp...  12.2 us

commit v1 on v0

--- a/solution.py
+++ b/solution.py
@@ -30,7 +30,6 @@
 MATRIX_RATE = 0.2
 STAT_DECAY = 0.5
 MASKED_SCORE = -1e30
-HIGHEST_PRECISION = lax.Precision.HIGHEST
 MIB = 1024 * 1024
 F32 = jnp.float32
 BF16 = jnp.bfloat16
@@ -841,10 +840,22 @@
         totals[index : index + 1, : VECTORS[index][1] * BLK] += column_sum(values)
 
     arrive(0)
-    branch = product(context_ref[...], w_out[...]) + vector(B_OUT)
-    unit_one, inverse_one = norm_parts(x_ref[...].astype(F32) + branch)
-    first = (unit_one * vector(GAIN_ONE) + vector(SHIFT_ONE)).astype(BF16)
-    first_ref[...] = first.T
+    sides = [slice(start, start + TILE // 2) for start in range(0, TILE, TILE // 2)]
+    units_one, inverses_one, firsts = [], [], []
+
+    def branch(index):
+        return product(context_ref[sides[index]], w_out[...])
+
+    def norm_first(index, values):
+        rows = sides[index]
+        unit, inverse = norm_parts(x_ref[rows].astype(F32) + (values + vector(B_OUT)))
+        units_one.append(unit)
+        inverses_one.append(inverse)
+        firsts.append((unit * vector(GAIN_ONE) + vector(SHIFT_ONE)).astype(BF16))
+        first_ref[:, rows] = firsts[-1].T
+
+    pipelined(2, branch, norm_first, lambda *_: None)
+    first = jnp.concatenate(firsts, axis=0)
     arrive(1)
     chunks = [slice(start, start + CHUNK) for start in range(0, FF, CHUNK)]
 
@@ -859,9 +870,19 @@
 
     pipelined(len(chunks), rise, bend, lambda *_: None)
     arrive(2, 3, 4)
-    downward = product(active_ref[...], w_down[...]) + vector(B_DOWN)
-    unit_two, inverse_two = norm_parts(first.astype(F32) + downward)
-    encoded = (unit_two * vector(GAIN_TWO) + vector(SHIFT_TWO)).astype(BF16)
+    units_two, inverses_two, encodeds = [], [], []
+
+    def sink(index):
+        return product(active_ref[sides[index]], w_down[...])
+
+    def norm_second(index, values):
+        unit, inverse = norm_parts(firsts[index].astype(F32) + (values + vector(B_DOWN)))
+        units_two.append(unit)
+        inverses_two.append(inverse)
+        encodeds.append((unit * vector(GAIN_TWO) + vector(SHIFT_TWO)).astype(BF16))
+
+    pipelined(2, sink, norm_second, lambda *_: None)
+    encoded = jnp.concatenate(encodeds, axis=0)
 
     @pl.when(tile < short_tiles)
     def _():
@@ -878,16 +899,16 @@
     def head():
         pooled = pooled_ref[...]
         wide_hidden = w_hidden[...].astype(F32)
-        hidden = jnp.tanh(product(pooled, wide_hidden, HIGHEST_PRECISION) + vector(B_HIDDEN))
-        logits = product(hidden, w_class[...], HIGHEST_PRECISION) + b_class[...]
+        hidden = jnp.tanh(product(pooled, wide_hidden) + vector(B_HIDDEN))
+        logits = product(hidden, w_class[...]) + b_class[...]
         d_logits = logit_cot[...]
         g_last[...] += column_sum(d_logits)
-        g_class[...] += left_product(d_logits, hidden, HIGHEST_PRECISION)
-        d_hidden = right_product(d_logits, w_class[...], HIGHEST_PRECISION)
+        g_class[...] += left_product(d_logits, hidden)
+        d_hidden = right_product(d_logits, w_class[...])
         d_hidden = d_hidden * (1.0 - hidden * hidden)
         add_total(B_HIDDEN, d_hidden)
-        g_hidden[...] += left_product(pooled, d_hidden, HIGHEST_PRECISION)
-        return logits, right_product(d_hidden, wide_hidden, HIGHEST_PRECISION)
+        g_hidden[...] += left_product(pooled, d_hidden)
+        return logits, right_product(d_hidden, wide_hidden)
 
     def pool(starts, size, lengths, cot_ref, logits_ref, first):
         count = len(starts)
@@ -927,14 +948,24 @@
     d_student = d_student_ref[...]
     add_total(B_STUDENT, d_student)
     g_student[...] += left_product(encoded, d_student)
-    cotangent = jnp.where(tile < short_tiles, cot_short_ref[...], cot_long_ref[...])
-    d_second = cotangent.astype(F32) + right_product(d_student, w_student[...])
-    add_total(GAIN_TWO, d_second * unit_two)
-    add_total(SHIFT_TWO, d_second)
-    d_resid_two = norm_back(d_second, vector(GAIN_TWO), unit_two, inverse_two)
-    d_down = d_resid_two.astype(BF16)
-    d_down_ref[...] = d_down.T
-    add_total(B_DOWN, d_down)
+    d_resids, d_downs = [], []
+
+    def through_student(index):
+        return right_product(d_student[sides[index]], w_student[...])
+
+    def norm_second_back(index, values):
+        rows = sides[index]
+        cotangent = jnp.where(tile < short_tiles, cot_short_ref[rows], cot_long_ref[rows])
+        d_second = cotangent.astype(F32) + values
+        add_total(GAIN_TWO, d_second * units_two[index])
+        add_total(SHIFT_TWO, d_second)
+        d_resids.append(norm_back(d_second, vector(GAIN_TWO), units_two[index], inverses_two[index]))
+        d_downs.append(d_resids[-1].astype(BF16))
+        d_down_ref[:, rows] = d_downs[-1].T
+        add_total(B_DOWN, d_downs[-1])
+
+    pipelined(2, through_student, norm_second_back, lambda *_: None)
+    d_down = jnp.concatenate(d_downs, axis=0)
 
     def fall(index):
         return right_product(d_down, w_down[chunks[index], :])
@@ -945,15 +976,26 @@
         totals[B_UP : B_UP + 1, chunks[index]] += column_sum(d_up)
 
     pipelined(len(chunks), fall, bend_back, lambda *_: None)
-    d_first = d_resid_two + right_product(d_up_ref[...], w_up[...])
-    add_total(GAIN_ONE, d_first * unit_one)
-    add_total(SHIFT_ONE, d_first)
-    d_resid_one = norm_back(d_first, vector(GAIN_ONE), unit_one, inverse_one)
-    d_resid_ref[...] = d_resid_one
-    d_branch = d_resid_one.astype(BF16)
-    d_branch_ref[...] = d_branch
-    add_total(B_OUT, d_branch)
-    d_context_ref[...] = right_product(d_branch, w_out[...]).astype(BF16)
+
+    def rise_back(index):
+        return right_product(d_up_ref[sides[index]], w_up[...])
+
+    def norm_first_back(index, values):
+        rows = sides[index]
+        d_first = d_resids[index] + values
+        add_total(GAIN_ONE, d_first * units_one[index])
+        add_total(SHIFT_ONE, d_first)
+        d_resid = norm_back(d_first, vector(GAIN_ONE), units_one[index], inverses_one[index])
+        d_resid_ref[rows] = d_resid
+        d_branch = d_resid.astype(BF16)
+        d_branch_ref[rows] = d_branch
+        add_total(B_OUT, d_branch)
+        return d_branch
+
+    def branch_back(index, d_branch):
+        d_context_ref[sides[index]] = right_product(d_branch, w_out[...]).astype(BF16)
+
+    pipelined(2, rise_back, norm_first_back, branch_back)
 
     @pl.when(tile == pl.num_programs(0) - 1)
     def _():

time: 405 us -> 389 us (0.960)
  Pallas kernels: 362 us -> 345 us
    pallas_call x1, Pallas kernels: 96.3 us -> 79.5 us  [feed(): pl.pallas_call(partial(feed_kernel, short_tiles=short_tiles, width=width)...]
where the time goes in v1:
time: 389 us; the launch traced here: 382 us
  Pallas kernels  345 us (89%)
  between operations  15.2 us (4%)
  local copies, waits for them, and re-layouts  11.9 us (3%)
  matrix products  5.55 us (1%)
  other arithmetic  4.58 us (1%)
    pallas_call x1, Pallas kernels, feed(): pl.pallas_call(partial(feed_kernel, short_tiles=short_tiles, width=width)...  79.5 us
    pallas_call x1, Pallas kernels, attention_back(): pl.pallas_call(partial(attention_back_kernel, short_tiles=short_tiles, tr...  62.5 us
    pallas_call x1, Pallas kernels, gather_shards(): pl.pallas_call(gather_kernel, in_specs=[pl.BlockSpec(memory_space=pltpu.V...  57.5 us
    pallas_call x1, Pallas kernels, reduce_late(): pl.pallas_call(partial(reduce_kernel, base=base, short_steps=short_steps)...  54.5 us
    pallas_call x1, Pallas kernels, attention(): pl.pallas_call(partial(attention_kernel, short_tiles=short_tiles), grid=(...  32.1 us
    pallas_call x1, Pallas kernels, feed_grads(): pl.pallas_call(feed_grads_kernel, grid_spec=pltpu.PrefetchScalarGridSpec(...  27.6 us
    pallas_call x1, Pallas kernels, update(): pl.pallas_call(update_kernel, grid_spec=pltpu.PrefetchScalarGridSpec(num_...  14.7 us
    pallas_call x1, Pallas kernels, input_weights(): pl.pallas_call(input_weights_kernel, grid_spec=pltpu.PrefetchScalarGridSp...  12.2 us

profile of v1, /device:TPU:8, one launch (start us, length us, event | category | flops | bytes accessed | tf_op | source)
XLA Modules:
  0.0 382.3 jit_solution(4974459604435969529)
XLA Ops:
  7.2 0.9 compare_reduce_fusion
  8.1 1.2 slice_bitcast_fusion.3.b_class_ref
  9.3 0.7 slice.27
  10.0 0.8 broadcast_multiply_fusion
  10.7 0.2 convert_reduce_fusion.1
  10.9 1.2 add_select_fusion.1
  12.8 0.7 slice.25
  13.5 1.4 pad_bitcast_fusion.params
  15.0 0.8 reshape.157.w_class_ref
  15.7 0.0 copy-start.6
  15.7 57.5 %gather.1 = bf16[8,7040,128]{2,1,0:T(8,128)(2,1)} custom-call(f32[7040,128]{1,0:T(8,128)} %bitcast.30), custom_call_target="tpu_custom_call" | custom-call | bytes 209715200 | tf_op jit(solution)/shard_map/gather/pallas_call | solution.py:1367
  73.2 0.0 copy-done.6
  73.2 4.3 %assemble.1.w_ref.refs_4_ = bf16[768,2304]{1,0:T(8,128)(2,1)} custom-call(s32[439]{0:T(512)S(1)} %copy-done.6, bf16[440,128,128]{2,1,0:T(8,128)(2,1)} %bitcast.28), custom_call_target="tpu_custom_call" | custom-call | tf_op jit(solution)/shard_map/assemble/pallas_call | solution.py:95
  77.5 32.1 %attention.1 = (bf16[2048,768]{1,0:T(8,128)(2,1)}, bf16[2048,768]{1,0:T(8,128)(2,1)}, bf16[2048,768]{1,0:T(8,128)(2,1)}, bf16[2048,768]{1,0:T(8,128)(2,1)}, bf16...) custom-call(s32[8]{0:T(128)} %len_short.3, s32[2]{0:T(128)} %len_long.3, ...), custom_call_target="tpu_custom_call" | custom-call | flops 10468982784 | bytes 36700160 | tf_op jit(solution)/shard_map/attention/pallas_call | solution.py:484
  109.7 79.5 %feed.1 = (bf16[1024,768]{1,0:T(8,128)(2,1)}, bf16[1024,768]{1,0:T(8,128)(2,1)}, f32[8,14]{1,0:T(8,128)}, f32[2,14]{1,0:T(2,128)}, bf16[768,2048]{1,0:T(8,128)(2...) custom-call(s32[8]{0:T(128)} %len_short.3, ...), custom_call_target="tpu_custom_call" | custom-call | flops 43486543872 | bytes 73400320 | tf_op jit(solution)/shard_map/feed/pallas_call | solution.py:1032
  189.2 0.0 copy-start.3
  189.2 0.0 copy-start.1
  189.2 5.6 %convolution_convert_fusion.g_out = bf16[768,768]{1,0:T(8,128)(2,1)S(1)} fusion(bf16[2048,768]{1,0:T(8,128)(2,1)} %get-tuple-element.136.context_ref, bf16[2048,768]{1,0:T(8,128)(2,1)} %get-tuple-element.151), kind=kOutput, calls=%fused_computation | convolution fusion | flops 2416508928 | bytes 7471104 | tf_op jit(solution)/shard_map/dot_general | solution.py:42
  194.8 0.0 copy-start.8
  194.8 0.0 copy-done.3
  194.8 0.0 copy-done.1
  194.9 0.0 copy-start.7
  194.9 27.6 %feed_grads.3._ = bf16[440,128,128]{2,1,0:T(8,128)(2,1)} custom-call(s32[439]{0:T(512)} %bitcast.34, bf16[768,2048]{1,0:T(8,128)(2,1)} %get-tuple-element.147.first_turned, bf16[768,2048]{1,0:T(8,128)(2,1)} %get-tuple-element.148.down_turned, bf16[2048,3072]{1,0:T(8,128)(2,1)} %get-tuple-element.149.active_ref, ...), custom_call_target="tpu_custom_call" | custom-call | flops 19327352832 | bytes 52428800 | tf_op jit(solution)/shard_map/feed_grads/pallas_call | solution.py:189
  222.5 0.0 copy-done.8
  222.5 0.0 copy-done.7
  222.5 62.5 %attention_back.1 = (bf16[2048,2304]{1,0:T(8,128)(2,1)}, f32[1,768]{1,0:T(1,128)S(1)}, f32[1,768]{1,0:T(1,128)S(1)}, bf16[768,2048]{1,0:T(8,128)(2,1)S(1)}, bf16[3968,128]{1,0:T(8,128)(2,1)}) custom-call(bf16[2048,768]{1,0:T(8,128)(2,1)} %get-tuple-element.141.refs_0_, bf16[2048,768]{1,0:T(8,128)(2,1)} %get-tuple-element.142.refs_1_, ...), custom_call_target="tpu_custom_call" | custom-call | flops 8053063680 | bytes 52428800 | tf_op jit(solution)/shard_map/attention_back/pallas_call | solution.py:639
  285.1 12.2 %input_weights.3 = (bf16[440,128,128]{2,1,0:T(8,128)(2,1)}, f32[96,128]{1,0:T(8,128)}) custom-call(s32[439]{0:T(512)} %bitcast.35, bf16[768,2048]{1,0:T(8,128)(2,1)S(1)} %get-tuple-element.154.turned, bf16[2048,2304]{1,0:T(8,128)(2,1)} %get-tuple-element.155.d_ref.refs_2_, ...), custom_call_target="tpu_custom_call", output_to_operand_aliasing={{0}: (6, {})} | custom-call | flops 7247757312 | bytes 16777216 | tf_op jit(solution)/shard_map/input_weights/pallas_call | solution.py:250
  297.3 54.5 %reduce.1 = (bf16[3072,128]{1,0:T(8,128)(2,1)}, f32[96,128]{1,0:T(8,128)}, f32[1024,768]{1,0:T(8,128)}, f32[1024,768]{1,0:T(8,128)}) custom-call(bf16[56320,128]{1,0:T(8,128)(2,1)} %bitcast.27, f32[96,128]{1,0:T(8,128)} %get-tuple-element.160.refs_1_, bf16[2048,2304]{1,0:T(8,128)(2,1)} %get-tuple-element.155.d_ref.refs_2_, ...), custom_call_target="tpu_custom_call" | custom-call | bytes 209715200 | tf_op jit(solution)/shard_map/reduce/pallas_call | solution.py:1669
  351.8 0.0 copy-start.4
  351.8 0.0 copy-start.2
  351.9 0.0 copy-start.5
  351.9 16.0 %conditional.1 = ((f32[55,128,128]{2,1,0:T(8,128)}, f32[55,128,128]{2,1,0:T(8,128)}, f32[55,128,128]{2,1,0:T(8,128)}, f32[55,128,128]{2,1,0:T(8,128)})) conditional(s32[]{:T(128)} %convert_element_type.32, (s32[439]{0:T(512)S(1)}, bf16[768,2048]{1,0:T(8,128)(2,1)}, bf16[768,2048]{1,0:T(8,128)(2,1)}, bf16[2048,3072]{1,0:T(8,128)(2,1)}, ...), branch_computations={%region_5.8_spmd, %region_8.9_spmd} | conditional | flops 27498758144 | bytes 161120576 | solution.py:1925
  351.9 1.3 slice.17.position_ref
  353.2 14.7 %update.3 = (f32[55,128,128]{2,1,0:T(8,128)}, f32[55,128,128]{2,1,0:T(8,128)}, f32[55,128,128]{2,1,0:T(8,128)}, f32[55,128,128]{2,1,0:T(8,128)}) custom-call(s32[55]{0:T(128)} %slice.17.position_ref, s32[55]{0:T(128)S(1)} %get-tuple-element.78.held_ref, bf16[3968,128]{1,0:T(8,128)(2,1)} %get-tuple-element.79.early, ...), custom_call_target="tpu_custom_call" | custom-call | flops 922746880 | bytes 32440320 | tf_op jit(solution)/shard_map/cond/branch_1_fun/update/pallas_call | solution.py:1775
  367.9 0.0 copy-done.4
  367.9 0.1 copy.33
  368.0 0.1 reshape.166
  368.2 0.0 copy-done.2
  368.2 0.0 copy-done.5
  368.2 1.5 divide_subtract_fusion
  369.7 0.0 copy-start
  369.7 3.9 %copy.47 = f32[8,128,768]{2,1,0:T(8,128)} copy(f32[8,128,768]{2,1,0:T(8,128)} %bitcast.32) | data formatting | bytes 6291456
  373.6 0.0 copy-done
  373.6 1.7 copy.48
  (8 shorter events, 0.1 us)
Async XLA Ops:
  15.7 57.5 %copy-start.6 = (s32[439]{0:T(512)S(1)}, s32[439]{0:T(512)}, u32[]{:S(2)}) copy-start(s32[439]{0:T(512)} %slot_ref.3) | copy-start | bytes 5272
  189.2 5.6 %copy-start.3 = (f32[128,128]{1,0:T(8,128)S(1)}, f32[128,128]{1,0:T(8,128)}, u32[]{:S(2)}) copy-start(f32[128,128]{1,0:T(8,128)} %get-tuple-element.153) | copy-start | bytes 196612
  189.2 5.6 %copy-start.1 = (f32[768,128]{1,0:T(8,128)S(1)}, f32[768,128]{1,0:T(8,128)}, u32[]{:S(2)}) copy-start(f32[768,128]{1,0:T(8,128)} %get-tuple-element.152) | copy-start | bytes 1179652
  194.8 27.7 %copy-start.8 = (bf16[768,768]{1,0:T(8,128)(2,1)}, bf16[768,768]{1,0:T(8,128)(2,1)S(1)}, u32[]{:S(2)}) copy-start(bf16[768,768]{1,0:T(8,128)(2,1)S(1)} %convolution_convert_fusion.g_out) | copy-start | bytes 3538948
  194.9 27.7 %copy-start.7 = (bf16[128,128]{1,0:T(8,128)(2,1)}, bf16[128,128]{1,0:T(8,128)(2,1)S(1)}, u32[]{:S(2)}) copy-start(bf16[128,128]{1,0:T(8,128)(2,1)S(1)} %convert_element_type.31.g_hidden) | copy-start | bytes 98308
  351.8 16.0 %copy-start.4 = (f32[96,128]{1,0:T(8,128)S(1)}, f32[96,128]{1,0:T(8,128)}, u32[]{:S(2)}) copy-start(f32[96,128]{1,0:T(8,128)} %get-tuple-element.170) | copy-start | bytes 147460
  351.8 16.3 %copy-start.2 = (f32[11406]{0:T(1024)S(1)}, f32[11406]{0:T(1024)}, u32[]{:S(2)}) copy-start(f32[11406]{0:T(1024)} %param.33) | copy-start | bytes 136876
  351.9 16.3 %copy-start.5 = (f32[11406]{0:T(1024)S(1)}, f32[11406]{0:T(1024)}, u32[]{:S(2)}) copy-start(f32[11406]{0:T(1024)} %param.35) | copy-start | bytes 136876
  369.7 3.9 %copy-start = (f32[1024,768]{1,0:T(8,128)S(1)}, f32[1024,768]{1,0:T(8,128)}, u32[]{:S(2)}) copy-start(f32[1024,768]{1,0:T(8,128)} %get-tuple-element.163) | copy-start | bytes 9437188

commit v2 on v1

--- a/solution.py
+++ b/solution.py
@@ -115,6 +115,7 @@
 
 
 PART = 512
+UNIT = 256
 ACROSS = PART // BLK
 
 
@@ -155,8 +156,24 @@
         wait_whole(up_stage.at[slot], up_sems.at[slot])
         wait_whole(down_stage.at[slot], down_sems.at[slot])
 
-    up_stage[slot] = product(first_turned[...], d_up_ref[...]).astype(BF16)
-    down_stage[slot] = product(down_turned[...], active_ref[...]).T.astype(BF16)
+
+    def keep_up(cols, values):
+        up_stage[slot, :, cols] = values.astype(BF16)
+
+    def keep_down(cols, values):
+        down_stage[slot, cols, :] = values.T.astype(BF16)
+
+    units = [slice(begin, begin + UNIT) for begin in range(0, PART, UNIT)]
+    in_turn(
+        [
+            (lambda cols=cols: product(first_turned[...], d_up_ref[:, cols]), partial(keep_up, cols))
+            for cols in units
+        ]
+        + [
+            (lambda cols=cols: product(down_turned[...], active_ref[:, cols]), partial(keep_down, cols))
+            for cols in units
+        ]
+    )
     for row in range(D // BLK):
         for col in range(ACROSS):
             pltpu.make_async_copy(
@@ -225,7 +242,13 @@
     def _():
         wait_whole(stage.at[slot], sems.at[slot])
 
-    stage[slot] = product(turned[...], d_ref[...]).astype(BF16)
+    def keep(cols, values):
+        stage[slot, :, cols] = values.astype(BF16)
+
+    units = [slice(begin, begin + UNIT) for begin in range(0, D, UNIT)]
+    in_turn(
+        [(lambda cols=cols: product(turned[...], d_ref[:, cols]), partial(keep, cols)) for cols in units]
+    )
     for row in range(D // BLK):
         for col in range(D // BLK):
             pltpu.make_async_copy(
@@ -306,6 +329,15 @@
             after(index - 1, done)
         done = middle(index, current)
     after(count - 1, done)
+
+
+def in_turn(stages):
+    pipelined(
+        len(stages),
+        lambda index: stages[index][0](),
+        lambda index, values: stages[index][1](values),
+        lambda *_: None,
+    )
 
 
 def softmax(scores, length):
@@ -839,7 +871,7 @@
     def add_total(index, values):
         totals[index : index + 1, : VECTORS[index][1] * BLK] += column_sum(values)
 
-    arrive(0)
+    arrive(0, 1, 2, 3, 4)
     sides = [slice(start, start + TILE // 2) for start in range(0, TILE, TILE // 2)]
     units_one, inverses_one, firsts = [], [], []
 
@@ -854,22 +886,19 @@
         firsts.append((unit * vector(GAIN_ONE) + vector(SHIFT_ONE)).astype(BF16))
         first_ref[:, rows] = firsts[-1].T
 
-    pipelined(2, branch, norm_first, lambda *_: None)
-    first = jnp.concatenate(firsts, axis=0)
-    arrive(1)
+
     chunks = [slice(start, start + CHUNK) for start in range(0, FF, CHUNK)]
 
-    def rise(index):
-        return product(first, w_up[:, chunks[index]])
-
-    def bend(index, upward):
-        upward = upward + vectors[B_UP : B_UP + 1, chunks[index]]
+    def rise(chunk, index):
+        return product(firsts[index], w_up[:, chunks[chunk]])
+
+    def bend(chunk, index, upward):
+        rows, cols = sides[index], chunks[chunk]
+        upward = upward + vectors[B_UP : B_UP + 1, cols]
         below, density = normal_parts(upward)
-        active_ref[:, chunks[index]] = (upward * below).astype(BF16)
-        slope[:, chunks[index]] = (below + upward * density).astype(BF16)
-
-    pipelined(len(chunks), rise, bend, lambda *_: None)
-    arrive(2, 3, 4)
+        active_ref[rows, cols] = (upward * below).astype(BF16)
+        slope[rows, cols] = (below + upward * density).astype(BF16)
+
     units_two, inverses_two, encodeds = [], [], []
 
     def sink(index):
@@ -881,7 +910,24 @@
         inverses_two.append(inverse)
         encodeds.append((unit * vector(GAIN_TWO) + vector(SHIFT_TWO)).astype(BF16))
 
-    pipelined(2, sink, norm_second, lambda *_: None)
+    students = []
+
+    def learn(index):
+        return product(encodeds[index], w_student[...])
+
+    def keep_student(index, values):
+        students.append(values + vector(B_STUDENT))
+
+    in_turn(
+        [(partial(branch, index), partial(norm_first, index)) for index in range(2)]
+        + [
+            (partial(rise, chunk, index), partial(bend, chunk, index))
+            for chunk in range(len(chunks))
+            for index in range(2)
+        ]
+        + [(partial(sink, index), partial(norm_second, index)) for index in range(2)]
+        + [(partial(learn, index), partial(keep_student, index)) for index in range(2)]
+    )
     encoded = jnp.concatenate(encodeds, axis=0)
 
     @pl.when(tile < short_tiles)
@@ -892,7 +938,7 @@
     def _():
         enc_long_ref[...] = encoded
 
-    student = product(encoded, w_student[...]) + vector(B_STUDENT)
+    student = jnp.concatenate(students, axis=0)
     query = vector(POOL_QUERY) * 0.125
     pooled_ref[...] = jnp.zeros_like(pooled_ref)
 
@@ -964,18 +1010,14 @@
         d_down_ref[:, rows] = d_downs[-1].T
         add_total(B_DOWN, d_downs[-1])
 
-    pipelined(2, through_student, norm_second_back, lambda *_: None)
-    d_down = jnp.concatenate(d_downs, axis=0)
-
-    def fall(index):
-        return right_product(d_down, w_down[chunks[index], :])
-
-    def bend_back(index, d_active):
-        d_up = (d_active * slope[:, chunks[index]].astype(F32)).astype(BF16)
-        d_up_ref[:, chunks[index]] = d_up
-        totals[B_UP : B_UP + 1, chunks[index]] += column_sum(d_up)
-
-    pipelined(len(chunks), fall, bend_back, lambda *_: None)
+    def fall(chunk, index):
+        return right_product(d_downs[index], w_down[chunks[chunk], :])
+
+    def bend_back(chunk, index, d_active):
+        rows, cols = sides[index], chunks[chunk]
+        d_up = (d_active * slope[rows, cols].astype(F32)).astype(BF16)
+        d_up_ref[rows, cols] = d_up
+        totals[B_UP : B_UP + 1, cols] += column_sum(d_up)
 
     def rise_back(index):
         return right_product(d_up_ref[sides[index]], w_up[...])
@@ -990,12 +1032,26 @@
         d_branch = d_resid.astype(BF16)
         d_branch_ref[rows] = d_branch
         add_total(B_OUT, d_branch)
-        return d_branch
-
-    def branch_back(index, d_branch):
-        d_context_ref[sides[index]] = right_product(d_branch, w_out[...]).astype(BF16)
-
-    pipelined(2, rise_back, norm_first_back, branch_back)
+        d_branches.append(d_branch)
+
+    d_branches = []
+
+    def branch_back(index):
+        return right_product(d_branches[index], w_out[...])
+
+    def keep_context(index, values):
+        d_context_ref[sides[index]] = values.astype(BF16)
+
+    in_turn(
+        [(partial(through_student, index), partial(norm_second_back, index)) for index in range(2)]
+        + [
+            (partial(fall, chunk, index), partial(bend_back, chunk, index))
+            for chunk in range(len(chunks))
+            for index in range(2)
+        ]
+        + [(partial(rise_back, index), partial(norm_first_back, index)) for index in range(2)]
+        + [(partial(branch_back, index), partial(keep_context, index)) for index in range(2)]
+    )
 
     @pl.when(tile == pl.num_programs(0) - 1)
     def _():

time: 389 us -> 390 us (level)
  no operation moved by 1% of the time
where the time goes in v2:
time: 390 us; the launch traced here: 384 us
  Pallas kernels  347 us (89%)
  between operations  15.2 us (4%)
  local copies, waits for them, and re-layouts  11.9 us (3%)
  matrix products  5.56 us (1%)
  other arithmetic  4.58 us (1%)
    pallas_call x1, Pallas kernels, feed(): pl.pallas_call(partial(feed_kernel, short_tiles=short_tiles, width=width)...  81 us
    pallas_call x1, Pallas kernels, attention_back(): pl.pallas_call(partial(attention_back_kernel, short_tiles=short_tiles, tr...  62.6 us
    pallas_call x1, Pallas kernels, gather_shards(): pl.pallas_call(gather_kernel, in_specs=[pl.BlockSpec(memory_space=pltpu.V...  57.5 us
    pallas_call x1, Pallas kernels, reduce_late(): pl.pallas_call(partial(reduce_kernel, base=base, short_steps=short_steps)...  54.5 us
    pallas_call x1, Pallas kernels, attention(): pl.pallas_call(partial(attention_kernel, short_tiles=short_tiles), grid=(...  32.1 us
    pallas_call x1, Pallas kernels, feed_grads(): pl.pallas_call(feed_grads_kernel, grid_spec=pltpu.PrefetchScalarGridSpec(...  27.8 us
    pallas_call x1, Pallas kernels, update(): pl.pallas_call(update_kernel, grid_spec=pltpu.PrefetchScalarGridSpec(num_...  14.7 us
    pallas_call x1, Pallas kernels, input_weights(): pl.pallas_call(input_weights_kernel, grid_spec=pltpu.PrefetchScalarGridSp...  12.2 us

profile of v2, /device:TPU:8, one launch (start us, length us, event | category | flops | bytes accessed | tf_op | source)
XLA Modules:
  0.0 384.0 jit_solution(2444700622277888301)
XLA Ops:
  7.2 0.9 compare_reduce_fusion
  8.1 1.2 slice_bitcast_fusion.3.b_class_ref
  9.3 0.7 slice.27
  10.0 0.8 broadcast_multiply_fusion
  10.7 0.2 convert_reduce_fusion.1
  10.9 1.2 add_select_fusion.1
  12.8 0.7 slice.25
  13.5 1.4 pad_bitcast_fusion.params
  15.0 0.8 reshape.157.w_class_ref
  15.7 0.0 copy-start.6
  15.7 57.5 %gather.1 = bf16[8,7040,128]{2,1,0:T(8,128)(2,1)} custom-call(f32[7040,128]{1,0:T(8,128)} %bitcast.30), custom_call_target="tpu_custom_call" | custom-call | bytes 209715200 | tf_op jit(solution)/shard_map/gather/pallas_call | solution.py:1423
  73.2 0.0 copy-done.6
  73.2 4.3 %assemble.1.w_ref.refs_4_ = bf16[768,2304]{1,0:T(8,128)(2,1)} custom-call(s32[439]{0:T(512)S(1)} %copy-done.6, bf16[440,128,128]{2,1,0:T(8,128)(2,1)} %bitcast.28), custom_call_target="tpu_custom_call" | custom-call | tf_op jit(solution)/shard_map/assemble/pallas_call | solution.py:95
  77.5 32.1 %attention.1 = (bf16[2048,768]{1,0:T(8,128)(2,1)}, bf16[2048,768]{1,0:T(8,128)(2,1)}, bf16[2048,768]{1,0:T(8,128)(2,1)}, bf16[2048,768]{1,0:T(8,128)(2,1)}, bf16...) custom-call(s32[8]{0:T(128)} %len_short.3, s32[2]{0:T(128)} %len_long.3, ...), custom_call_target="tpu_custom_call" | custom-call | flops 10468982784 | bytes 36700160 | tf_op jit(solution)/shard_map/attention/pallas_call | solution.py:516
  109.7 81.0 %feed.1 = (bf16[1024,768]{1,0:T(8,128)(2,1)}, bf16[1024,768]{1,0:T(8,128)(2,1)}, f32[8,14]{1,0:T(8,128)}, f32[2,14]{1,0:T(2,128)}, bf16[768,2048]{1,0:T(8,128)(2...) custom-call(s32[8]{0:T(128)} %len_short.3, ...), custom_call_target="tpu_custom_call" | custom-call | flops 43486543872 | bytes 73400320 | tf_op jit(solution)/shard_map/feed/pallas_call | solution.py:1088
  190.7 0.0 copy-start.3
  190.7 0.0 copy-start.1
  190.7 5.6 %convolution_convert_fusion.g_out = bf16[768,768]{1,0:T(8,128)(2,1)S(1)} fusion(bf16[2048,768]{1,0:T(8,128)(2,1)} %get-tuple-element.136.context_ref, bf16[2048,768]{1,0:T(8,128)(2,1)} %get-tuple-element.151), kind=kOutput, calls=%fused_computation | convolution fusion | flops 2416508928 | bytes 7471104 | tf_op jit(solution)/shard_map/dot_general | solution.py:42
  196.3 0.0 copy-start.8
  196.3 0.0 copy-done.3
  196.3 0.0 copy-done.1
  196.3 0.0 copy-start.7
  196.4 27.8 %feed_grads.3._ = bf16[440,128,128]{2,1,0:T(8,128)(2,1)} custom-call(s32[439]{0:T(512)} %bitcast.34, bf16[768,2048]{1,0:T(8,128)(2,1)} %get-tuple-element.147.first_turned, bf16[768,2048]{1,0:T(8,128)(2,1)} %get-tuple-element.148.down_turned, bf16[2048,3072]{1,0:T(8,128)(2,1)} %get-tuple-element.149.active_ref, ...), custom_call_target="tpu_custom_call" | custom-call | flops 19327352832 | bytes 52428800 | tf_op jit(solution)/shard_map/feed_grads/pallas_call | solution.py:206
  224.2 0.0 copy-done.8
  224.2 0.0 copy-done.7
  224.2 62.6 %attention_back.1 = (bf16[2048,2304]{1,0:T(8,128)(2,1)}, f32[1,768]{1,0:T(1,128)S(1)}, f32[1,768]{1,0:T(1,128)S(1)}, bf16[768,2048]{1,0:T(8,128)(2,1)S(1)}, bf16[3968,128]{1,0:T(8,128)(2,1)}) custom-call(bf16[2048,768]{1,0:T(8,128)(2,1)} %get-tuple-element.141.refs_0_, bf16[2048,768]{1,0:T(8,128)(2,1)} %get-tuple-element.142.refs_1_, ...), custom_call_target="tpu_custom_call" | custom-call | flops 8053063680 | bytes 52428800 | tf_op jit(solution)/shard_map/attention_back/pallas_call | solution.py:671
  286.7 12.2 %input_weights.3 = (bf16[440,128,128]{2,1,0:T(8,128)(2,1)}, f32[96,128]{1,0:T(8,128)}) custom-call(s32[439]{0:T(512)} %bitcast.35, bf16[768,2048]{1,0:T(8,128)(2,1)S(1)} %get-tuple-element.154.turned, bf16[2048,2304]{1,0:T(8,128)(2,1)} %get-tuple-element.155.d_ref.refs_2_, ...), custom_call_target="tpu_custom_call", output_to_operand_aliasing={{0}: (6, {})} | custom-call | flops 7247757312 | bytes 16777216 | tf_op jit(solution)/shard_map/input_weights/pallas_call | solution.py:273
  299.0 54.5 %reduce.1 = (bf16[3072,128]{1,0:T(8,128)(2,1)}, f32[96,128]{1,0:T(8,128)}, f32[1024,768]{1,0:T(8,128)}, f32[1024,768]{1,0:T(8,128)}) custom-call(bf16[56320,128]{1,0:T(8,128)(2,1)} %bitcast.27, f32[96,128]{1,0:T(8,128)} %get-tuple-element.160.refs_1_, bf16[2048,2304]{1,0:T(8,128)(2,1)} %get-tuple-element.155.d_ref.refs_2_, ...), custom_call_target="tpu_custom_call" | custom-call | bytes 209715200 | tf_op jit(solution)/shard_map/reduce/pallas_call | solution.py:1725
  353.5 0.0 copy-start.4
  353.5 0.0 copy-start.2
  353.5 0.0 copy-start.5
  353.5 16.0 %conditional.1 = ((f32[55,128,128]{2,1,0:T(8,128)}, f32[55,128,128]{2,1,0:T(8,128)}, f32[55,128,128]{2,1,0:T(8,128)}, f32[55,128,128]{2,1,0:T(8,128)})) conditional(s32[]{:T(128)} %convert_element_type.32, (s32[439]{0:T(512)S(1)}, bf16[768,2048]{1,0:T(8,128)(2,1)}, bf16[768,2048]{1,0:T(8,128)(2,1)}, bf16[2048,3072]{1,0:T(8,128)(2,1)}, ...), branch_computations={%region_5.8_spmd, %region_8.9_spmd} | conditional | flops 27498758144 | bytes 161120576 | solution.py:1981
  353.6 1.3 slice.17.position_ref
  354.8 14.7 %update.3 = (f32[55,128,128]{2,1,0:T(8,128)}, f32[55,128,128]{2,1,0:T(8,128)}, f32[55,128,128]{2,1,0:T(8,128)}, f32[55,128,128]{2,1,0:T(8,128)}) custom-call(s32[55]{0:T(128)} %slice.17.position_ref, s32[55]{0:T(128)S(1)} %get-tuple-element.78.held_ref, bf16[3968,128]{1,0:T(8,128)(2,1)} %get-tuple-element.79.early, ...), custom_call_target="tpu_custom_call" | custom-call | flops 922746880 | bytes 32440320 | tf_op jit(solution)/shard_map/cond/branch_1_fun/update/pallas_call | solution.py:1831
  369.6 0.0 copy-done.4
  369.6 0.1 copy.33
  369.7 0.1 reshape.166
  369.9 0.0 copy-done.2
  369.9 0.0 copy-done.5
  369.9 1.5 divide_subtract_fusion
  371.3 0.0 copy-start
  371.3 3.9 %copy.47 = f32[8,128,768]{2,1,0:T(8,128)} copy(f32[8,128,768]{2,1,0:T(8,128)} %bitcast.32) | data formatting | bytes 6291456
  375.3 0.0 copy-done
  375.3 1.7 copy.48
  (8 shorter events, 0.1 us)
Async XLA Ops:
  15.7 57.5 %copy-start.6 = (s32[439]{0:T(512)S(1)}, s32[439]{0:T(512)}, u32[]{:S(2)}) copy-start(s32[439]{0:T(512)} %slot_ref.3) | copy-start | bytes 5272
  190.7 5.6 %copy-start.3 = (f32[128,128]{1,0:T(8,128)S(1)}, f32[128,128]{1,0:T(8,128)}, u32[]{:S(2)}) copy-start(f32[128,128]{1,0:T(8,128)} %get-tuple-element.153) | copy-start | bytes 196612
  190.7 5.6 %copy-start.1 = (f32[768,128]{1,0:T(8,128)S(1)}, f32[768,128]{1,0:T(8,128)}, u32[]{:S(2)}) copy-start(f32[768,128]{1,0:T(8,128)} %get-tuple-element.152) | copy-start | bytes 1179652
  196.3 27.9 %copy-start.8 = (bf16[768,768]{1,0:T(8,128)(2,1)}, bf16[768,768]{1,0:T(8,128)(2,1)S(1)}, u32[]{:S(2)}) copy-start(bf16[768,768]{1,0:T(8,128)(2,1)S(1)} %convolution_convert_fusion.g_out) | copy-start | bytes 3538948
  196.3 27.8 %copy-start.7 = (bf16[128,128]{1,0:T(8,128)(2,1)}, bf16[128,128]{1,0:T(8,128)(2,1)S(1)}, u32[]{:S(2)}) copy-start(bf16[128,128]{1,0:T(8,128)(2,1)S(1)} %convert_element_type.31.g_hidden) | copy-start | bytes 98308
  353.5 16.0 %copy-start.4 = (f32[96,128]{1,0:T(8,128)S(1)}, f32[96,128]{1,0:T(8,128)}, u32[]{:S(2)}) copy-start(f32[96,128]{1,0:T(8,128)} %get-tuple-element.170) | copy-start | bytes 147460
  353.5 16.3 %copy-start.2 = (f32[11406]{0:T(1024)S(1)}, f32[11406]{0:T(1024)}, u32[]{:S(2)}) copy-start(f32[11406]{0:T(1024)} %param.33) | copy-start | bytes 136876
  353.5 16.3 %copy-start.5 = (f32[11406]{0:T(1024)S(1)}, f32[11406]{0:T(1024)}, u32[]{:S(2)}) copy-start(f32[11406]{0:T(1024)} %param.35) | copy-start | bytes 136876
  371.3 3.9 %copy-start = (f32[1024,768]{1,0:T(8,128)S(1)}, f32[1024,768]{1,0:T(8,128)}, u32[]{:S(2)}) copy-start(f32[1024,768]{1,0:T(8,128)} %get-tuple-element.163) | copy-start | bytes 9437188
